TPU v7x, 256 devices: a whole 4x4x8 slice. The times are simulated.
256 devices in a mesh: gx: 8 (over z), gy: 4 (over y), gz: 8 (over x, core).
Axes of the slice: x: 4, y: 4, z: 8, core: 2. Of those that a mesh axis runs over, the one named last changes fastest.
Arguments:
- subspace: bfloat16 [64, 192, 256, 128], P('gx', 'gy', 'gz'), may hold values from -45 to 45, as said below
- potential: float32 [64, 192, 256], P('gx', 'gy', 'gz'), may hold values from -3 to 1
Outputs:
- density: float32 [64, 192, 256], P('gx', 'gy', 'gz')
- energy_density: float32 [64, 192, 256], P('gx', 'gy', 'gz')
Inputs may be any that keep to these rules, and one draw needn't show every extreme that they name: `subspace`: vectors 0 to 63 are the current orbitals, vectors 64 to 127 the preconditioned residuals.
All inputs are finite; a program needn't handle non-finite values.
Results may differ from a plain program's by a relative error of at most 0.0045.
Values may be sent and summed in bfloat16 or wider, within the bound.
A program may use at most 64 MiB of HBM per device.

v0:
```python
import jax
import jax.numpy as jnp
from jax import lax
from jax.sharding import PartitionSpec as P

NB = 64
FILTER_STEPS = 8


stencil = (-1.0 / 12.0, 4.0 / 3.0, -2.5, 4.0 / 3.0, -1.0 / 12.0)


def with_halo(block, sides, width):
    for axis, dim in sides:
        count = lax.axis_size(axis)
        forward = [(i, i + 1) for i in range(count - 1)]
        backward = [(target, source) for source, target in forward]
        low = lax.ppermute(
            lax.slice_in_dim(block, block.shape[dim] - width, None, axis=dim), axis, forward
        )
        high = lax.ppermute(lax.slice_in_dim(block, 0, width, axis=dim), axis, backward)
        block = jnp.concatenate([low, block, high], axis=dim)
    return block


def second_diff(values, axis_id):
    count = values.shape[axis_id] - 4
    total = stencil[0] * lax.slice_in_dim(values, 0, count, axis=axis_id).astype(jnp.float32)
    for offset in range(1, 5):
        total = total + stencil[offset] * lax.slice_in_dim(
            values, offset, offset + count, axis=axis_id
        ).astype(jnp.float32)
    return total


def make_projector(correlation, hamil):
    identity = jnp.eye(correlation.shape[0], dtype=jnp.float32)
    symmetric = 0.5 * (hamil + hamil.T)
    factor = jnp.linalg.cholesky(correlation)
    left_solve = lax.linalg.triangular_solve(factor, symmetric, left_side=True, lower=True)
    reduced = lax.linalg.triangular_solve(factor, left_solve.T, left_side=True, lower=True)
    reduced = 0.5 * (reduced + reduced.T)
    shifted = reduced - jnp.trace(reduced) / reduced.shape[0] * identity
    sign_matrix = shifted / jnp.sqrt(jnp.sum(shifted * shifted) + 1e-06)
    for repeat in range(FILTER_STEPS):
        square = jnp.dot(sign_matrix, sign_matrix, precision=lax.Precision.HIGHEST)
        sign_matrix = 1.5 * sign_matrix - 0.5 * jnp.dot(
            square, sign_matrix, precision=lax.Precision.HIGHEST
        )
    projector = 0.5 * (identity - sign_matrix)
    half_solve = lax.linalg.triangular_solve(
        factor, projector, left_side=True, lower=True, transpose_a=True
    )
    rotation = lax.linalg.triangular_solve(
        factor, half_solve.T, left_side=True, lower=True, transpose_a=True
    )
    return (0.5 * (rotation + rotation.T)).astype(jnp.bfloat16)


def body(subspace, potential):
    width = subspace.shape[3]
    ncell = float(
        subspace.shape[0]
        * subspace.shape[1]
        * subspace.shape[2]
        * lax.axis_size("gx")
        * lax.axis_size("gy")
        * lax.axis_size("gz")
    )
    contract = (((0,), (0,)), ((), ()))
    flat = subspace.reshape(-1, width)
    extended = with_halo(subspace, (("gx", 0), ("gy", 1), ("gz", 2)), 2)
    laplace = (
        second_diff(extended[:, 2:-2, 2:-2], 0)
        + second_diff(extended[2:-2, :, 2:-2], 1)
        + second_diff(extended[2:-2, 2:-2, :], 2)
    )
    applied = (-0.5 * laplace + potential[..., None] * subspace.astype(jnp.float32)).astype(
        jnp.bfloat16
    )
    applied_flat = applied.reshape(-1, width)
    local_hamil = lax.dot_general(flat, applied_flat, contract, preferred_element_type=jnp.float32)
    local_over = lax.dot_general(flat, flat, contract, preferred_element_type=jnp.float32)
    correlation, hamil = lax.psum((local_over, local_hamil), ("gx", "gy", "gz"))
    rotation = make_projector(correlation / ncell, hamil / ncell)
    mixed = jnp.dot(flat, rotation, preferred_element_type=jnp.float32)
    charge = jnp.sum(flat.astype(jnp.float32) * mixed, axis=1) / NB
    energy = jnp.sum(applied_flat.astype(jnp.float32) * mixed, axis=1) / NB
    return (charge.reshape(potential.shape), energy.reshape(potential.shape))


def solution(mesh):
    return jax.shard_map(
        body,
        mesh=mesh,
        in_specs=(P("gx", "gy", "gz", None), P("gx", "gy", "gz")),
        out_specs=(P("gx", "gy", "gz"), P("gx", "gy", "gz")),
        check_vma=False,
    )
```

profile of v0, /device:TPU:1, one launch (start us, length us, event | category | flops | bytes accessed | tf_op | source)
XLA Modules:
  0.0 382.5 jit_solution(2450044555730156935)
XLA Ops:
  7.2 1.8 fusion.52
  9.0 4.4 %collective-permute-start = (bf16[2,48,32,128]{3,2,1,0:T(8,128)(2,1)S(1)}, bf16[2,48,32,128]{3,2,1,0:T(8,128)(2,1)S(1)}, u32[]{:S(2)}, u32[]{:S(2)}) collective-permute-start(bf16[2,48,32,128]{3,2,1,0:T(8,128)(2,1)S(1)} %get-tuple-element.20), channel_id=1, source_target_pairs={{0,32},{32,64},{64,96},{96,128},{128,160},{160,192},{192,224},{1,3... | collective-permute-start | bytes 2359304 | tf_op jit(solution)/shard_map/ppermute | solution.py:18
  13.5 1.3 collective-permute-start.1
  14.8 14.8 %collective-permute-done = bf16[2,48,32,128]{3,2,1,0:T(8,128)(2,1)S(1)} collective-permute-done((bf16[2,48,32,128]{3,2,1,0:T(8,128)(2,1)S(1)}, bf16[2,48,32,128]{3,2,1,0:T(8,128)(2,1)S(1)}, u32[]{:S(2)}, u32[]{:S(2)}) %collective-permute-start) | collective-permute-done | bytes 786464 | tf_op jit(solution)/shard_map/ppermute | solution.py:18
  29.6 0.3 constant_dynamic-update-slice_fusion.1
  29.9 2.6 constant_dynamic-update-slice_fusion
  32.5 1.2 collective-permute-done.1
  33.8 0.3 constant_dynamic-update-slice_fusion.2
  34.1 2.1 copy-done.1
  36.2 1.4 fusion.51
  37.6 3.2 collective-permute-start.2
  40.9 1.3 collective-permute-start.3
  42.2 1.7 copy.25
  43.9 2.8 copy.18
  46.7 0.8 collective-permute-done.3
  47.5 2.6 pad_maximum_fusion.10
  50.0 6.2 %collective-permute-start.4 = (bf16[12,52,2,128]{3,2,1,0:T(2,128)(2,1)S(1)}, bf16[12,52,2,128]{3,2,1,0:T(2,128)(2,1)S(1)}, u32[]{:S(2)}, u32[]{:S(2)}) collective-permute-start(bf16[12,52,2,128]{3,2,1,0:T(2,128)(2,1)S(1)} %get-tuple-element.12), channel_id=1, source_target_pairs={{0,1},{1,2},{2,3},{3,4},{4,5},{5,6},{6,7},{8,9},{9,10},{10,11},{11... | collective-permute-start | bytes 958472 | tf_op jit(solution)/shard_map/ppermute | solution.py:18
  56.2 1.9 collective-permute-start.5
  58.2 1.7 convolution_bitcast_fusion.4
  59.8 0.3 collective-permute-done.4
  60.1 4.4 %collective-permute-done.5 = bf16[12,52,2,128]{3,2,1,0:T(2,128)(2,1)S(1)} collective-permute-done((bf16[12,52,2,128]{3,2,1,0:T(2,128)(2,1)S(1)}, bf16[12,52,2,128]{3,2,1,0:T(2,128)(2,1)S(1)}, u32[]{:S(2)}, u32[]{:S(2)}) %collective-permute-start.5) | collective-permute-done | bytes 319520 | tf_op jit(solution)/shard_map/ppermute | solution.py:21
  64.5 22.5 %fusion.9 = bf16[8,48,32,128]{3,2,1,0:T(8,128)(2,1)S(1)} fusion(bf16[8,48,32,128]{3,2,1,0:T(8,128)(2,1)S(1)} %copy-done, bf16[12,48,32,128]{3,2,1,0:T(8,128)(2,1)} %copy-done.1, bf16[12,2,32,128]{3,2,1,0:T(8,128)(2,1)S(1)} %collective-permute-done.3, bf16[12,2,32,128]{3,2,1,0:T(8,128)(2,1)S(1)} %collective-permute-done.2, ...), kind=kLoop, calls=%fused_computation.12 | loop fusion | flops 132120576 | bytes 24674304 | tf_op jit(solution)/shard_map/convert_element_type | solution.py:78
  87.1 1.6 copy-done.7
  88.7 1.7 convolution_bitcast_fusion.3
  90.5 4.2 %bitcast_convert_fusion = f32[12288,128]{1,0:T(8,128)} fusion(bf16[8,48,32,128]{3,2,1,0:T(8,128)(2,1)} %copy-done.7), kind=kLoop, calls=%fused_computation.33 | loop fusion | flops 1572864 | bytes 9437184 | tf_op jit(solution)/shard_map/convert_element_type | solution.py:88
  94.7 6.6 %copy.31 = f32[12288,128]{0,1:T(8,128)} copy(f32[12288,128]{1,0:T(8,128)} %bitcast_convert_fusion) | data formatting | bytes 12582912 | tf_op jit(solution)/shard_map/convert_element_type | solution.py:88
  101.3 233.2 %all-reduce.3.cloned.1.call-done = (f32[128,128]{0,1:T(8,128)}, f32[128,128]{0,1:T(8,128)}) async-done(((f32[128,128]{0,1:T(8,128)}, f32[128,128]{0,1:T(8,128)}), (f32[128,128]{0,1:T(8,128)}, f32[128,128]{0,1:T(8,128)})) %all-reduce.3.cloned.1.call-update) | async-done | bytes 131088 | tf_op jit(solution)/shard_map/psum | solution.py:84
  334.6 0.8 broadcast_multiply_fusion.1
  335.5 0.9 fusion.38
  336.5 11.7 %cholesky.24 = f32[128,128]{1,0:T(8,128)S(1)} custom-call(f32[128,128]{1,0:T(8,128)S(1)} %copy.24), custom_call_target="Cholesky" | custom-call | tf_op jit(solution)/shard_map/jit(cholesky)/cholesky | solution.py:39
  348.3 0.6 compare_reduce_fusion
  348.9 0.7 fusion.26
  349.6 9.8 %custom-call.14 = f32[1,128,128]{1,2,0:T(8,128)S(1)} custom-call(f32[1,128,128]{2,1,0:T(8,128)S(1)} %fusion.26), custom_call_target="InvertDiagBlocksLowerTriangular" | custom-call | tf_op jit(solution)/shard_map/triangular_solve/custom-call.2 | solution.py:54
  359.5 1.1 convolution_bitcast_fusion.2
  360.6 0.3 fusion.33
  361.0 0.6 select_reduce_fusion
  362.3 0.6 multiply_reduce_fusion.2
  363.6 0.2 fusion.43
  363.8 0.2 fusion.25
  364.3 0.2 fusion.24
  365.5 0.2 fusion.21
  366.8 0.2 fusion.18
  367.2 0.3 fusion.36
  367.6 1.0 convolution_bitcast_fusion
  368.6 0.9 copy-done.6
  369.5 4.4 %multiply_reduce_fusion = (f32[12288]{0:T(1024)S(1)}, f32[12288]{0:T(1024)S(1)}) fusion(f32[12288,128]{0,1:T(8,128)} %copy.31, f32[12288,128]{0,1:T(8,128)S(1)} %convolution_bitcast_fusion, bf16[12288,128]{0,1:T(8,128)(2,1)S(1)} %copy-done.6), kind=kLoop, calls=%fused_computation.17 | loop fusion | flops 7839744 | bytes 15826944 | tf_op jit(solution)/shard_map/reduce_sum | solution.py:88
  374.0 0.8 copy.32
  374.9 0.8 copy.33
  (40 shorter events, 3.2 us)
Async XLA Ops:
  7.2 22.7 %copy-start = (bf16[8,48,32,128]{3,2,1,0:T(8,128)(2,1)S(1)}, bf16[8,48,32,128]{3,2,1,0:T(8,128)(2,1)}, u32[]{:S(2)}) copy-start(bf16[8,48,32,128]{3,2,1,0:T(8,128)(2,1)} %param.6) | copy-start | bytes 9437188
  7.2 327.4 %all-reduce.3.cloned.1.call-start = ((), (), s32[]{:S(2)}) async-start(), calls=%async_computation | async-start | bytes 262144 | tf_op jit(solution)/shard_map/psum | solution.py:84
  9.0 20.6 %collective-permute-start = (bf16[2,48,32,128]{3,2,1,0:T(8,128)(2,1)S(1)}, bf16[2,48,32,128]{3,2,1,0:T(8,128)(2,1)S(1)}, u32[]{:S(2)}, u32[]{:S(2)}) collective-permute-start(bf16[2,48,32,128]{3,2,1,0:T(8,128)(2,1)S(1)} %get-tuple-element.20), channel_id=1, source_target_pairs={{0,32},{32,64},{64,96},{96,128},{128,160},{160,192},{192,224},{1,3... | collective-permute-start | bytes 2359304 | tf_op jit(solution)/shard_map/ppermute | solution.py:18
  13.5 20.3 %collective-permute-start.1 = (bf16[2,48,32,128]{3,2,1,0:T(8,128)(2,1)S(1)}, bf16[2,48,32,128]{3,2,1,0:T(8,128)(2,1)S(1)}, u32[]{:S(2)}, u32[]{:S(2)}) collective-permute-start(bf16[2,48,32,128]{3,2,1,0:T(8,128)(2,1)S(1)} %get-tuple-element.19), channel_id=1, source_target_pairs={{32,0},{64,32},{96,64},{128,96},{160,128},{192,160},{224,192},{33,... | collective-permute-start | bytes 2359304 | tf_op jit(solution)/shard_map/ppermute | solution.py:21
  32.5 5.1 %copy-start.4 = (bf16[10,48,32,128]{3,2,1,0:T(8,128)(2,1)}, bf16[10,48,32,128]{3,2,1,0:T(8,128)(2,1)S(1)}, u32[]{:S(2)}) copy-start(bf16[10,48,32,128]{3,2,1,0:T(8,128)(2,1)S(1)} %get-tuple-element.16) | copy-start | bytes 11796484
  34.1 2.1 copy-start.1
  34.1 3.5 copy-start.2
  37.6 9.1 %collective-permute-start.2 = (bf16[12,2,32,128]{3,2,1,0:T(8,128)(2,1)}, bf16[12,2,32,128]{3,2,1,0:T(8,128)(2,1)S(1)}, u32[]{:S(2)}, u32[]{:S(2)}) collective-permute-start(bf16[12,2,32,128]{3,2,1,0:T(8,128)(2,1)} %get-tuple-element.14), channel_id=1, source_target_pairs={{0,8},{8,16},{16,24},{1,9},{9,17},{17,25},{2,10},{10,18},{18,26},{... | collective-permute-start | bytes 589832 | tf_op jit(solution)/shard_map/ppermute | solution.py:18
  40.9 6.6 %collective-permute-start.3 = (bf16[12,2,32,128]{3,2,1,0:T(8,128)(2,1)}, bf16[12,2,32,128]{3,2,1,0:T(8,128)(2,1)S(1)}, u32[]{:S(2)}, u32[]{:S(2)}) collective-permute-start(bf16[12,2,32,128]{3,2,1,0:T(8,128)(2,1)} %get-tuple-element.15), channel_id=1, source_target_pairs={{8,0},{16,8},{24,16},{9,1},{17,9},{25,17},{10,2},{18,10},{26,18},{... | collective-permute-start | bytes 589832 | tf_op jit(solution)/shard_map/ppermute | solution.py:21
  46.7 17.8 %copy-start.3 = (bf16[10,48,32,128]{3,2,1,0:T(8,128)(2,1)S(1)}, bf16[10,48,32,128]{3,2,1,0:T(8,128)(2,1)}, u32[]{:S(2)}) copy-start(bf16[10,48,32,128]{3,2,1,0:T(8,128)(2,1)} %copy-done.2) | copy-start | bytes 11796484
  46.7 17.8 %copy-start.5 = (bf16[10,48,32,128]{3,2,1,0:T(8,128)(2,1)S(1)}, bf16[10,48,32,128]{3,2,1,0:T(8,128)(2,1)}, u32[]{:S(2)}) copy-start(bf16[10,48,32,128]{3,2,1,0:T(8,128)(2,1)} %copy-done.4) | copy-start | bytes 11796484
  46.7 17.8 %copy-start.8 = (f32[8,48,32]{2,1,0:T(8,128)S(1)}, f32[8,48,32]{2,1,0:T(8,128)}, u32[]{:S(2)}) copy-start(f32[8,48,32]{2,1,0:T(8,128)} %copy.25) | copy-start | bytes 147460
  50.0 10.1 %collective-permute-start.4 = (bf16[12,52,2,128]{3,2,1,0:T(2,128)(2,1)S(1)}, bf16[12,52,2,128]{3,2,1,0:T(2,128)(2,1)S(1)}, u32[]{:S(2)}, u32[]{:S(2)}) collective-permute-start(bf16[12,52,2,128]{3,2,1,0:T(2,128)(2,1)S(1)} %get-tuple-element.12), channel_id=1, source_target_pairs={{0,1},{1,2},{2,3},{3,4},{4,5},{5,6},{6,7},{8,9},{9,10},{10,11},{11... | collective-permute-start | bytes 958472 | tf_op jit(solution)/shard_map/ppermute | solution.py:18
  56.2 8.3 %collective-permute-start.5 = (bf16[12,52,2,128]{3,2,1,0:T(2,128)(2,1)S(1)}, bf16[12,52,2,128]{3,2,1,0:T(2,128)(2,1)S(1)}, u32[]{:S(2)}, u32[]{:S(2)}) collective-permute-start(bf16[12,52,2,128]{3,2,1,0:T(2,128)(2,1)S(1)} %get-tuple-element.13), channel_id=1, source_target_pairs={{1,0},{2,1},{3,2},{4,3},{5,4},{6,5},{7,6},{9,8},{10,9},{11,10},{12... | collective-permute-start | bytes 958472 | tf_op jit(solution)/shard_map/ppermute | solution.py:21
  87.1 1.6 copy-start.7
  367.6 1.9 copy-start.6
Sparse Core Ops, SparseCore 0:
  90.6 243.9 all-reduce.2
where the time goes:
time: 383 us; the launch traced here: 382 us
  waiting for transfers between devices  255 us (67%)
  other arithmetic  59.5 us (16%)
  local copies, waits for them, and re-layouts  24.4 us (6%)
  starting transfers between devices  18.3 us (5%)
  between operations  15.8 us (4%)
  matrix products  9.58 us (3%)
    psum x1, waiting for transfers between devices, body(): correlation, hamil = lax.psum((local_over, local_hamil), ('gx', 'gy', 'gz'))  233 us
    convert_element_type x1, other arithmetic, body(): (-0.5 * laplace + potential[..., None] * subspace.astype(jnp.float32)).as...  22.5 us
    ppermute x3, waiting for transfers between devices, with_halo(): lax.ppermute(lax.slice_in_dim(block, block.shape[dim] - width, None, axis...  15.1 us
    ppermute x3, starting transfers between devices, with_halo(): lax.ppermute(lax.slice_in_dim(block, block.shape[dim] - width, None, axis...  13.8 us
    another operation x3, other arithmetic, make_projector(): factor = jnp.linalg.cholesky(correlation)  12.4 us
    another operation x2, other arithmetic, make_projector(): lax.linalg.triangular_solve(factor, half_solve.T, left_side=True, lower=T...  10.5 us
    unnamed x22, local copies, waits for them, and re-layouts  8.17 us
  transfers between devices with their start and end apart: 7, of which 6 were waited for; matrix products, arithmetic and copies ran while one was open for 5% of the time, Pallas kernels for 0%

commit v1 on v0

--- a/solution.py
+++ b/solution.py
@@ -1,10 +1,13 @@
 import jax
 import jax.numpy as jnp
 from jax import lax
+from jax.experimental import pallas as pl
+from jax.experimental.pallas import tpu as pltpu
 from jax.sharding import PartitionSpec as P
 
 NB = 64
 FILTER_STEPS = 8
+MESH = pl.DeviceIdType.MESH
 
 
 stencil = (-1.0 / 12.0, 4.0 / 3.0, -2.5, 4.0 / 3.0, -1.0 / 12.0)
@@ -31,6 +34,90 @@
             values, offset, offset + count, axis=axis_id
         ).astype(jnp.float32)
     return total
+
+
+AXES = ("gx", "gy", "gz")
+
+
+def place(axis, index):
+    return tuple(index if name == axis else lax.axis_index(name) for name in AXES)
+
+
+def all_reduce_kernel(sizes, x_ref, o_ref, part, got_z, got_x, got_y, send_sem, recv_sem):
+    rows = part.shape[0]
+    nx, ny, nz = sizes
+    me = {name: lax.axis_index(name) for name in AXES}
+    size = dict(zip(AXES, sizes))
+
+    barrier = pltpu.get_barrier_semaphore()
+    for axis in AXES:
+        for off in range(1, size[axis]):
+            peer = lax.rem(me[axis] + off, size[axis])
+            pl.semaphore_signal(barrier, inc=1, device_id=place(axis, peer), device_id_type=MESH)
+    pl.semaphore_wait(barrier, nx + ny + nz - 3)
+
+    def exchange(stage, axis, source, target):
+        copies = []
+        for off in range(1, size[axis]):
+            peer = lax.rem(me[axis] + off, size[axis])
+            copy = pltpu.make_async_remote_copy(
+                src_ref=source(peer),
+                dst_ref=target,
+                send_sem=send_sem.at[stage],
+                recv_sem=recv_sem.at[stage],
+                device_id=place(axis, peer),
+                device_id_type=MESH,
+            )
+            copy.start()
+            copies.append(copy)
+        return copies
+
+    def finish(stage, count, like):
+        whole = like.at[pl.ds(0, count)]
+        pltpu.make_async_copy(whole, whole, recv_sem.at[stage]).wait()
+        pltpu.make_async_copy(whole, whole, send_sem.at[stage]).wait()
+
+    exchange(0, "gz", lambda peer: x_ref.at[peer], got_z.at[me["gz"]])
+    got_z[me["gz"]] = x_ref[me["gz"]]
+    finish(0, nz - 1, got_z)
+    part[...] = sum(got_z[i] for i in range(1, nz)) + got_z[0]
+
+    exchange(1, "gy", lambda peer: part, got_y.at[me["gy"]])
+    got_y[me["gy"]] = part[...]
+    finish(1, ny - 1, got_y)
+    part2 = sum(got_y[i] for i in range(1, ny)) + got_y[0]
+    got_x[me["gx"]] = part2
+
+    exchange(2, "gx", lambda peer: got_x.at[me["gx"]], got_x.at[me["gx"]])
+    finish(2, nx - 1, got_x)
+    o_ref[me["gz"]] = sum(got_x[i] for i in range(1, nx)) + got_x[0]
+
+    exchange(3, "gz", lambda peer: o_ref.at[me["gz"]], o_ref.at[me["gz"]])
+    finish(3, nz - 1, o_ref)
+
+
+def all_reduce(value):
+    sizes = tuple(lax.axis_size(name) for name in AXES)
+    nx, ny, nz = sizes
+    rows = value.shape[0] // nz
+    import functools
+
+    out = pl.pallas_call(
+        functools.partial(all_reduce_kernel, sizes),
+        out_shape=jax.ShapeDtypeStruct((nz, rows, value.shape[1]), jnp.float32),
+        in_specs=[pl.BlockSpec(memory_space=pltpu.VMEM)],
+        out_specs=pl.BlockSpec(memory_space=pltpu.VMEM),
+        scratch_shapes=[
+            pltpu.VMEM((rows, value.shape[1]), jnp.float32),
+            pltpu.VMEM((nz, rows, value.shape[1]), jnp.float32),
+            pltpu.VMEM((nx, rows, value.shape[1]), jnp.float32),
+            pltpu.VMEM((ny, rows, value.shape[1]), jnp.float32),
+            pltpu.SemaphoreType.DMA((4,)),
+            pltpu.SemaphoreType.DMA((4,)),
+        ],
+        compiler_params=pltpu.CompilerParams(collective_id=0, has_side_effects=True),
+    )(value.reshape(nz, rows, value.shape[1]))
+    return out.reshape(value.shape)
 
 
 def make_projector(correlation, hamil):
@@ -81,7 +168,8 @@
     applied_flat = applied.reshape(-1, width)
     local_hamil = lax.dot_general(flat, applied_flat, contract, preferred_element_type=jnp.float32)
     local_over = lax.dot_general(flat, flat, contract, preferred_element_type=jnp.float32)
-    correlation, hamil = lax.psum((local_over, local_hamil), ("gx", "gy", "gz"))
+    both = all_reduce(jnp.concatenate([local_over, local_hamil], axis=0))
+    correlation, hamil = both[:width], both[width:]
     rotation = make_projector(correlation / ncell, hamil / ncell)
     mixed = jnp.dot(flat, rotation, preferred_element_type=jnp.float32)
     charge = jnp.sum(flat.astype(jnp.float32) * mixed, axis=1) / NB

time: 383 us -> 161 us (0.42)
  waiting for transfers between devices: 255 us -> 22.2 us
  Pallas kernels: 0 us -> 27.7 us
  between operations: 15.8 us -> 2.44 us
    psum x1 -> x0, waiting for transfers between devices: 233 us -> none  [body(): correlation, hamil = lax.psum((local_over, local_hamil), ('gx', 'gy', 'gz'))]
    pallas_call x0 -> x1, Pallas kernels: none -> 27.7 us  [all_reduce(): pl.pallas_call(functools.partial(all_reduce_kernel, sizes), out_shape=jax...]
    unnamed x22 -> x24, local copies, waits for them, and re-layouts: 8.17 us -> 5.69 us
  transfers between devices with their start and end apart: 7 -> 6, of which waited for: 6 -> 5; matrix products, arithmetic and copies ran while one was open for 5% -> 5% of each run, Pallas kernels for 0% -> 0%
where the time goes in v1:
time: 161 us; the launch traced here: 160 us
  other arithmetic  57.4 us (36%)
  Pallas kernels  27.7 us (17%)
  waiting for transfers between devices  22.2 us (14%)
  local copies, waits for them, and re-layouts  21.9 us (14%)
  starting transfers between devices  18.7 us (12%)
  matrix products  10.1 us (6%)
  between operations  2.44 us (2%)
    pallas_call x1, Pallas kernels, all_reduce(): pl.pallas_call(functools.partial(all_reduce_kernel, sizes), out_shape=jax...  27.7 us
    convert_element_type x1, other arithmetic, body(): (-0.5 * laplace + potential[..., None] * subspace.astype(jnp.float32)).as...  20.7 us
    ppermute x3, waiting for transfers between devices, with_halo(): lax.ppermute(lax.slice_in_dim(block, block.shape[dim] - width, None, axis...  15.4 us
    ppermute x3, starting transfers between devices, with_halo(): lax.ppermute(lax.slice_in_dim(block, block.shape[dim] - width, None, axis...  13.8 us
    another operation x3, other arithmetic, make_projector(): factor = jnp.linalg.cholesky(correlation)  12.4 us
    another operation x2, other arithmetic, make_projector(): lax.linalg.triangular_solve(factor, half_solve.T, left_side=True, lower=T...  10.5 us
    ppermute x3, waiting for transfers between devices, with_halo(): lax.ppermute(lax.slice_in_dim(block, 0, width, axis=dim), axis, backward)  6.86 us
    convert_element_type x1, local copies, waits for them, and re-layouts, body(): energy = jnp.sum(applied_flat.astype(jnp.float32) * mixed, axis=1) / NB  6.75 us
  transfers between devices with their start and end apart: 6, of which 5 were waited for; matrix products, arithmetic and copies ran while one was open for 5% of the time, Pallas kernels for 0%

profile of v1, /device:TPU:1, one launch (start us, length us, event | category | flops | bytes accessed | tf_op | source)
XLA Modules:
  0.0 160.4 jit_solution(8658924843129496250)
XLA Ops:
  0.6 1.8 %fusion.52 = (bf16[2,48,32,128]{3,2,1,0:T(8,128)(2,1)S(1)}, bf16[2,48,32,128]{3,2,1,0:T(8,128)(2,1)S(1)}) fusion(bf16[8,48,32,128]{3,2,1,0:T(8,128)(2,1)} %param.6), kind=kLoop, calls=%fused_computation.104 | loop fusion | bytes 3145728 | tf_op jit(solution)/shard_map/slice | solution.py:24
  2.5 4.4 %collective-permute-start = (bf16[2,48,32,128]{3,2,1,0:T(8,128)(2,1)S(1)}, bf16[2,48,32,128]{3,2,1,0:T(8,128)(2,1)S(1)}, u32[]{:S(2)}, u32[]{:S(2)}) collective-permute-start(bf16[2,48,32,128]{3,2,1,0:T(8,128)(2,1)S(1)} %get-tuple-element.18), channel_id=1, source_target_pairs={{0,32},{32,64},{64,96},{96,128},{128,160},{160,192},{192,224},{1,3... | collective-permute-start | bytes 2359304 | tf_op jit(solution)/shard_map/ppermute | solution.py:21
  6.9 1.3 collective-permute-start.1
  8.2 14.8 %collective-permute-done = bf16[2,48,32,128]{3,2,1,0:T(8,128)(2,1)S(1)} collective-permute-done((bf16[2,48,32,128]{3,2,1,0:T(8,128)(2,1)S(1)}, bf16[2,48,32,128]{3,2,1,0:T(8,128)(2,1)S(1)}, u32[]{:S(2)}, u32[]{:S(2)}) %collective-permute-start) | collective-permute-done | bytes 786464 | tf_op jit(solution)/shard_map/ppermute | solution.py:21
  23.0 0.3 constant_dynamic-update-slice_fusion.1
  23.3 2.6 %constant_dynamic-update-slice_fusion = (bf16[10,48,32,128]{3,2,1,0:T(8,128)(2,1)S(1)}, bf16[10,48,32,128]{3,2,1,0:T(8,128)(2,1)S(1)}, bf16[12,48,32,128]{3,2,1,0:T(8,128)(2,1)S(1)}) fusion(bf16[10,48,32,128]{3,2,1,0:T(8,128)(2,1)S(1)} %get-tuple-element.19, bf16[8,48,32,128]{3,2,1,0:T(8,128)(2,1)S(1)} %copy-done, ...), kind=kLoop, calls=%fused_computation.90 | loop fusion | bytes 12582912 | tf_op jit(solution)/shard_map/concatenate | solution.py:25
  25.9 1.2 collective-permute-done.1
  27.2 0.3 constant_dynamic-update-slice_fusion.2
  27.5 2.1 %copy-done.1 = bf16[12,48,32,128]{3,2,1,0:T(8,128)(2,1)} copy-done((bf16[12,48,32,128]{3,2,1,0:T(8,128)(2,1)}, bf16[12,48,32,128]{3,2,1,0:T(8,128)(2,1)S(1)}, u32[]{:S(2)}) %copy-start.1) | copy-done | bytes 4718616
  29.7 1.4 fusion.51
  31.0 3.2 %collective-permute-start.2 = (bf16[12,2,32,128]{3,2,1,0:T(8,128)(2,1)}, bf16[12,2,32,128]{3,2,1,0:T(8,128)(2,1)S(1)}, u32[]{:S(2)}, u32[]{:S(2)}) collective-permute-start(bf16[12,2,32,128]{3,2,1,0:T(8,128)(2,1)} %get-tuple-element.12), channel_id=1, source_target_pairs={{0,8},{8,16},{16,24},{1,9},{9,17},{17,25},{2,10},{10,18},{18,26},{... | collective-permute-start | bytes 589832 | tf_op jit(solution)/shard_map/ppermute | solution.py:21
  34.2 1.3 collective-permute-start.3
  35.5 1.7 %copy.20 = f32[8,48,32]{2,1,0:T(8,128)} copy(f32[8,48,32]{1,2,0:T(8,128)} %param.7) | data formatting | bytes 98304 | tf_op args[1]
  37.2 2.8 %copy.17 = bf16[12288,128]{0,1:T(8,128)(2,1)} copy(bf16[12288,128]{1,0:T(8,128)(2,1)S(1)} %bitcast.99) | data formatting | bytes 6291456 | tf_op jit(solution)/shard_map/reshape | solution.py:158
  40.1 0.8 collective-permute-done.3
  40.9 2.2 %pad_maximum_fusion.10 = (bf16[12,52,2,128]{3,2,1,0:T(2,128)(2,1)S(1)}, bf16[12,52,2,128]{3,2,1,0:T(2,128)(2,1)S(1)}) fusion(bf16[12,2,32,128]{3,2,1,0:T(8,128)(2,1)S(1)} %collective-permute-done.3, bf16[12,48,32,128]{3,2,1,0:T(8,128)(2,1)} %copy-done.1, bf16[12,2,32,128]{3,2,1,0:T(8,128)(2,1)S(1)} %collective-permute-done.2), kind=kLoop, calls=%fused_computation.58 | loop fusion | flops 1916928 | bytes 5750784 | tf_op jit(solution)/shard_map/slice | solution.py:22
  43.0 6.1 %collective-permute-start.4 = (bf16[12,52,2,128]{3,2,1,0:T(2,128)(2,1)S(1)}, bf16[12,52,2,128]{3,2,1,0:T(2,128)(2,1)S(1)}, u32[]{:S(2)}, u32[]{:S(2)}) collective-permute-start(bf16[12,52,2,128]{3,2,1,0:T(2,128)(2,1)S(1)} %get-tuple-element.10), channel_id=1, source_target_pairs={{0,1},{1,2},{2,3},{3,4},{4,5},{5,6},{6,7},{8,9},{9,10},{10,11},{11... | collective-permute-start | bytes 958472 | tf_op jit(solution)/shard_map/ppermute | solution.py:21
  49.2 2.3 %collective-permute-start.5 = (bf16[12,52,2,128]{3,2,1,0:T(2,128)(2,1)S(1)}, bf16[12,52,2,128]{3,2,1,0:T(2,128)(2,1)S(1)}, u32[]{:S(2)}, u32[]{:S(2)}) collective-permute-start(bf16[12,52,2,128]{3,2,1,0:T(2,128)(2,1)S(1)} %get-tuple-element.11), channel_id=1, source_target_pairs={{1,0},{2,1},{3,2},{4,3},{5,4},{6,5},{7,6},{9,8},{10,9},{11,10},{12... | collective-permute-start | bytes 958472 | tf_op jit(solution)/shard_map/ppermute | solution.py:24
  51.6 1.0 convolution_bitcast_fusion.4
  52.6 0.5 collective-permute-done.4
  53.1 4.8 %collective-permute-done.5 = bf16[12,52,2,128]{3,2,1,0:T(2,128)(2,1)S(1)} collective-permute-done((bf16[12,52,2,128]{3,2,1,0:T(2,128)(2,1)S(1)}, bf16[12,52,2,128]{3,2,1,0:T(2,128)(2,1)S(1)}, u32[]{:S(2)}, u32[]{:S(2)}) %collective-permute-start.5) | collective-permute-done | bytes 319520 | tf_op jit(solution)/shard_map/ppermute | solution.py:24
  58.0 20.7 %fusion.9 = bf16[8,48,32,128]{3,2,1,0:T(8,128)(2,1)S(1)} fusion(bf16[8,48,32,128]{3,2,1,0:T(8,128)(2,1)S(1)} %copy-done, bf16[12,48,32,128]{3,2,1,0:T(8,128)(2,1)S(1)} %bitcast.102, bf16[12,2,32,128]{3,2,1,0:T(8,128)(2,1)S(1)} %collective-permute-done.3, bf16[12,2,32,128]{3,2,1,0:T(8,128)(2,1)S(1)} %collective-permute-done.2, ...), kind=kLoop, calls=%fused_computation.12 | loop fusion | flops 132120576 | bytes 24674304 | tf_op jit(solution)/shard_map/convert_element_type | solution.py:165
  78.7 1.1 convolution_bitcast_fusion.3
  79.8 2.9 %bitcast_convert_fusion = f32[12288,128]{1,0:T(8,128)} fusion(bf16[8,48,32,128]{3,2,1,0:T(8,128)(2,1)S(1)} %fusion.9), kind=kLoop, calls=%fused_computation.33 | loop fusion | flops 1572864 | bytes 9437184 | tf_op jit(solution)/shard_map/convert_element_type | solution.py:176
  82.7 0.7 pad_maximum_fusion.11
  83.4 27.7 %shard_map.41 = f32[8,32,128]{2,1,0:T(8,128)} custom-call(f32[8,32,128]{2,1,0:T(8,128)} %bitcast.106), custom_call_target="tpu_custom_call" | custom-call | tf_op jit(solution)/shard_map/pallas_call | solution.py:105
  111.0 0.9 slice_multiply_fusion.1
  112.0 11.7 %cholesky.24 = f32[128,128]{1,0:T(8,128)S(1)} custom-call(f32[128,128]{1,0:T(8,128)S(1)} %fusion.38), custom_call_target="Cholesky" | custom-call | tf_op jit(solution)/shard_map/jit(cholesky)/cholesky | solution.py:126
  123.8 0.6 compare_reduce_fusion
  124.4 0.7 fusion.26
  125.1 9.8 %custom-call.14 = f32[1,128,128]{1,2,0:T(8,128)S(1)} custom-call(f32[1,128,128]{2,1,0:T(8,128)S(1)} %fusion.26), custom_call_target="InvertDiagBlocksLowerTriangular" | custom-call | tf_op jit(solution)/shard_map/triangular_solve/custom-call.2 | solution.py:141
  135.0 0.3 convolution_bitcast_fusion.2
  135.3 0.3 fusion.33
  135.7 0.6 select_reduce_fusion
  137.0 0.6 multiply_reduce_fusion.2
  138.3 0.2 fusion.43
  138.5 0.2 fusion.25
  138.9 0.2 fusion.24
  139.4 0.2 fusion.23
  139.8 0.2 fusion.22
  140.2 0.2 fusion.21
  141.5 0.2 fusion.18
  141.9 0.3 fusion.36
  142.3 3.6 %convolution_bitcast_fusion = f32[12288,128]{0,1:T(8,128)} fusion(bf16[12288,128]{1,0:T(8,128)(2,1)S(1)} %bitcast.100, f32[128,128]{1,0:T(8,128)S(1)} %fusion.36, f32[128,128]{0,1:T(8,128)S(1)} %copy.26), kind=kOutput, calls=%fused_computation | convolution fusion | flops 402702336 | bytes 9568256 | tf_op jit(solution)/shard_map/dot_general | solution.py:174
  145.9 6.8 %copy.27 = f32[12288,128]{0,1:T(8,128)} copy(f32[12288,128]{1,0:T(8,128)} %bitcast_convert_fusion) | data formatting | bytes 12582912 | tf_op jit(solution)/shard_map/convert_element_type | solution.py:176
  152.6 6.0 %multiply_reduce_fusion = (f32[12288]{0:T(1024)S(1)}, f32[12288]{0:T(1024)S(1)}) fusion(f32[12288,128]{0,1:T(8,128)} %copy.27, f32[12288,128]{0,1:T(8,128)} %convolution_bitcast_fusion, bf16[12288,128]{0,1:T(8,128)(2,1)S(1)} %copy-done.6), kind=kLoop, calls=%fused_computation.17 | loop fusion | flops 7839744 | bytes 15826944 | tf_op jit(solution)/shard_map/reduce_sum | solution.py:176
  158.7 0.8 copy.28
  159.6 0.8 copy.29
  (40 shorter events, 2.7 us)
Async XLA Ops:
  0.6 22.7 %copy-start = (bf16[8,48,32,128]{3,2,1,0:T(8,128)(2,1)S(1)}, bf16[8,48,32,128]{3,2,1,0:T(8,128)(2,1)}, u32[]{:S(2)}) copy-start(bf16[8,48,32,128]{3,2,1,0:T(8,128)(2,1)} %param.6) | copy-start | bytes 9437188
  2.5 20.6 %collective-permute-start = (bf16[2,48,32,128]{3,2,1,0:T(8,128)(2,1)S(1)}, bf16[2,48,32,128]{3,2,1,0:T(8,128)(2,1)S(1)}, u32[]{:S(2)}, u32[]{:S(2)}) collective-permute-start(bf16[2,48,32,128]{3,2,1,0:T(8,128)(2,1)S(1)} %get-tuple-element.18), channel_id=1, source_target_pairs={{0,32},{32,64},{64,96},{96,128},{128,160},{160,192},{192,224},{1,3... | collective-permute-start | bytes 2359304 | tf_op jit(solution)/shard_map/ppermute | solution.py:21
  6.9 20.3 %collective-permute-start.1 = (bf16[2,48,32,128]{3,2,1,0:T(8,128)(2,1)S(1)}, bf16[2,48,32,128]{3,2,1,0:T(8,128)(2,1)S(1)}, u32[]{:S(2)}, u32[]{:S(2)}) collective-permute-start(bf16[2,48,32,128]{3,2,1,0:T(8,128)(2,1)S(1)} %get-tuple-element.17), channel_id=1, source_target_pairs={{32,0},{64,32},{96,64},{128,96},{160,128},{192,160},{224,192},{33,... | collective-permute-start | bytes 2359304 | tf_op jit(solution)/shard_map/ppermute | solution.py:24
  25.9 5.1 %copy-start.4 = (bf16[10,48,32,128]{3,2,1,0:T(8,128)(2,1)}, bf16[10,48,32,128]{3,2,1,0:T(8,128)(2,1)S(1)}, u32[]{:S(2)}) copy-start(bf16[10,48,32,128]{3,2,1,0:T(8,128)(2,1)S(1)} %get-tuple-element.14) | copy-start | bytes 11796484
  27.5 2.1 %copy-start.1 = (bf16[12,48,32,128]{3,2,1,0:T(8,128)(2,1)}, bf16[12,48,32,128]{3,2,1,0:T(8,128)(2,1)S(1)}, u32[]{:S(2)}) copy-start(bf16[12,48,32,128]{3,2,1,0:T(8,128)(2,1)S(1)} %get-tuple-element.22) | copy-start | bytes 14155780
  27.5 3.5 %copy-start.2 = (bf16[10,48,32,128]{3,2,1,0:T(8,128)(2,1)}, bf16[10,48,32,128]{3,2,1,0:T(8,128)(2,1)S(1)}, u32[]{:S(2)}) copy-start(bf16[10,48,32,128]{3,2,1,0:T(8,128)(2,1)S(1)} %get-tuple-element.21) | copy-start | bytes 11796484
  31.0 9.0 %collective-permute-start.2 = (bf16[12,2,32,128]{3,2,1,0:T(8,128)(2,1)}, bf16[12,2,32,128]{3,2,1,0:T(8,128)(2,1)S(1)}, u32[]{:S(2)}, u32[]{:S(2)}) collective-permute-start(bf16[12,2,32,128]{3,2,1,0:T(8,128)(2,1)} %get-tuple-element.12), channel_id=1, source_target_pairs={{0,8},{8,16},{16,24},{1,9},{9,17},{17,25},{2,10},{10,18},{18,26},{... | collective-permute-start | bytes 589832 | tf_op jit(solution)/shard_map/ppermute | solution.py:21
  34.2 6.6 %collective-permute-start.3 = (bf16[12,2,32,128]{3,2,1,0:T(8,128)(2,1)}, bf16[12,2,32,128]{3,2,1,0:T(8,128)(2,1)S(1)}, u32[]{:S(2)}, u32[]{:S(2)}) collective-permute-start(bf16[12,2,32,128]{3,2,1,0:T(8,128)(2,1)} %get-tuple-element.13), channel_id=1, source_target_pairs={{8,0},{16,8},{24,16},{9,1},{17,9},{25,17},{10,2},{18,10},{26,18},{... | collective-permute-start | bytes 589832 | tf_op jit(solution)/shard_map/ppermute | solution.py:24
  43.0 10.1 %collective-permute-start.4 = (bf16[12,52,2,128]{3,2,1,0:T(2,128)(2,1)S(1)}, bf16[12,52,2,128]{3,2,1,0:T(2,128)(2,1)S(1)}, u32[]{:S(2)}, u32[]{:S(2)}) collective-permute-start(bf16[12,52,2,128]{3,2,1,0:T(2,128)(2,1)S(1)} %get-tuple-element.10), channel_id=1, source_target_pairs={{0,1},{1,2},{2,3},{3,4},{4,5},{5,6},{6,7},{8,9},{9,10},{10,11},{11... | collective-permute-start | bytes 958472 | tf_op jit(solution)/shard_map/ppermute | solution.py:21
  49.2 8.8 %slice-start = ((s8[4718592]{0:T(1024)(128)(4,1)}), s8[4194304]{0:T(1024)(128)(4,1)S(1)}, s32[]{:S(2)}) async-start(s8[4718592]{0:T(1024)(128)(4,1)} %bitcast.101), calls=%async_computation | async-start | bytes 8388608
  49.2 8.7 %slice-start.1 = ((s8[4718592]{0:T(1024)(128)(4,1)}), s8[524288]{0:T(1024)(128)(4,1)S(1)}, s32[]{:S(2)}) async-start(s8[4718592]{0:T(1024)(128)(4,1)} %bitcast.101), calls=%async_computation.1 | async-start | bytes 1048576
  49.2 8.7 %copy-start.3 = (bf16[10,48,32,128]{3,2,1,0:T(8,128)(2,1)S(1)}, bf16[10,48,32,128]{3,2,1,0:T(8,128)(2,1)}, u32[]{:S(2)}) copy-start(bf16[10,48,32,128]{3,2,1,0:T(8,128)(2,1)} %copy-done.2) | copy-start | bytes 11796484
  49.2 8.7 %copy-start.5 = (bf16[10,48,32,128]{3,2,1,0:T(8,128)(2,1)S(1)}, bf16[10,48,32,128]{3,2,1,0:T(8,128)(2,1)}, u32[]{:S(2)}) copy-start(bf16[10,48,32,128]{3,2,1,0:T(8,128)(2,1)} %copy-done.4) | copy-start | bytes 11796484
  49.2 8.7 %copy-start.7 = (f32[8,48,32]{2,1,0:T(8,128)S(1)}, f32[8,48,32]{2,1,0:T(8,128)}, u32[]{:S(2)}) copy-start(f32[8,48,32]{2,1,0:T(8,128)} %copy.20) | copy-start | bytes 147460
  49.2 8.7 %collective-permute-start.5 = (bf16[12,52,2,128]{3,2,1,0:T(2,128)(2,1)S(1)}, bf16[12,52,2,128]{3,2,1,0:T(2,128)(2,1)S(1)}, u32[]{:S(2)}, u32[]{:S(2)}) collective-permute-start(bf16[12,52,2,128]{3,2,1,0:T(2,128)(2,1)S(1)} %get-tuple-element.11), channel_id=1, source_target_pairs={{1,0},{2,1},{3,2},{4,3},{5,4},{6,5},{7,6},{9,8},{10,9},{11,10},{12... | collective-permute-start | bytes 958472 | tf_op jit(solution)/shard_map/ppermute | solution.py:24
  145.9 6.8 %copy-start.6 = (bf16[12288,128]{0,1:T(8,128)(2,1)S(1)}, bf16[12288,128]{0,1:T(8,128)(2,1)}, u32[]{:S(2)}) copy-start(bf16[12288,128]{0,1:T(8,128)(2,1)} %copy.17) | copy-start | bytes 9437188

commit v2 on v0

v2 whole, which is shorter than its diff:
```python
import functools

import jax
import jax.numpy as jnp
from jax import lax
from jax.experimental import pallas as pl
from jax.experimental.pallas import tpu as pltpu
from jax.sharding import PartitionSpec as P

NB = 64
FILTER_STEPS = 8
MESH = pl.DeviceIdType.MESH
AXES = ("gx", "gy", "gz")
F32, BF16 = jnp.float32, jnp.bfloat16

CX, CY, CZ, NV = 8, 48, 32, 128
CELLS = CX * CZ
HALF = CY // 2
LOADS = 4
PIECES = 4
LATE = 2
ZPIECES = 2


def place(axis, index):
    return tuple(index if name == axis else lax.axis_index(name) for name in AXES)


def iota(shape, dim):
    return lax.broadcasted_iota(jnp.int32, shape, dim)


def tap(distance):
    return jnp.where(distance == 1, 16.0, 0.0) - jnp.where(distance == 2, 1.0, 0.0)


def dot_nn(a, b):
    return jnp.dot(a, b, preferred_element_type=F32)


def dot_nt(a, b):
    return lax.dot_general(a, b, (((1,), (1,)), ((), ())), preferred_element_type=F32)


def exact(a, b):
    return jnp.dot(a, b, precision=lax.Precision.HIGHEST, preferred_element_type=F32)


def exact_nt(a, b):
    return lax.dot_general(
        a, b, (((1,), (1,)), ((), ())), precision=lax.Precision.HIGHEST, preferred_element_type=F32
    )


def kernel(
    sizes, u_hbm, pot_hbm, dens_out, en_out,
    u_v, ut, appl, hx, hy, hz, zs, xc, potv, pott, at, ez, bt, bg, pz, eye,
    c_in, c_z, c_y, c_x, c_out, h_in, h_z, h_y, h_x, h_out, mat, linv, linvt, rows_d, rows_e,
    load_sem, x_send, x_recv, y_send, y_recv, z_send, z_recv, ar_send, ar_recv,
):
    size = dict(zip(AXES, sizes))
    me = {name: lax.axis_index(name) for name in AXES}
    gx, gy, gz = me["gx"], me["gy"], me["gz"]
    nx, ny, nz = sizes
    ncell = float(nx * ny * nz * CX * CY * CZ)

    per = CY // LOADS
    loads = []
    for i in range(LOADS):
        span = pl.ds(i * per, per)
        loads.append(pltpu.make_async_copy(u_hbm.at[:, span], u_v.at[:, span], load_sem.at[i]))
        loads[-1].start()
    pot_load = pltpu.make_async_copy(pot_hbm, potv, load_sem.at[LOADS])
    pot_load.start()

    barrier = pltpu.get_barrier_semaphore()
    for axis in AXES:
        for off in range(1, size[axis]):
            peer = lax.rem(me[axis] + off, size[axis])
            pl.semaphore_signal(barrier, inc=1, device_id=place(axis, peer), device_id_type=MESH)
    pl.semaphore_wait(barrier, nx + ny + nz - 3)

    def send(src, dst, ssem, rsem, axis, peer):
        return pltpu.make_async_remote_copy(
            src_ref=src, dst_ref=dst, send_sem=ssem, recv_sem=rsem,
            device_id=place(axis, peer), device_id_type=MESH,
        )

    def x_copy(side, start, count, slot):
        layers = pl.ds(CX - 2, 2) if side == 0 else pl.ds(0, 2)
        span = pl.ds(start, count)
        peer = lax.rem(gx + 1, nx) if side == 0 else lax.rem(gx + nx - 1, nx)
        return send(
            u_hbm.at[layers, span], hx.at[side, :, span],
            x_send.at[side, slot], x_recv.at[side, slot], "gx", peer,
        )

    early_n, late_n = HALF // PIECES, HALF // LATE

    def x_early(side, i):
        return x_copy(side, (HALF if side == 0 else 0) + i * early_n, early_n, i)

    def x_late(side, i):
        return x_copy(side, (0 if side == 0 else HALF) + i * late_n, late_n, PIECES + i)

    def y_copy(side):
        layers = pl.ds(CY - 2, 2) if side == 0 else pl.ds(0, 2)
        peer = lax.rem(gy + 1, ny) if side == 0 else lax.rem(gy + ny - 1, ny)
        return send(
            u_hbm.at[:, layers], hy.at[side], y_send.at[side], y_recv.at[side], "gy", peer
        )

    def z_copy(side, i):
        span = pl.ds(i * (CY // ZPIECES), CY // ZPIECES)
        peer = lax.rem(gz + 1, nz) if side == 0 else lax.rem(gz + nz - 1, nz)
        return send(
            zs.at[span, side], hz.at[span, side],
            z_send.at[side, i], z_recv.at[side, i], "gz", peer,
        )

    def sends(axis, side):
        return me[axis] < size[axis] - 1 if side == 0 else me[axis] > 0

    def receives(axis, side):
        return me[axis] > 0 if side == 0 else me[axis] < size[axis] - 1

    for side in range(2):
        @pl.when(sends("gy", side))
        def _():
            y_copy(side).start()

    for i in range(PIECES):
        for side in range(2):
            @pl.when(sends("gx", side))
            def _():
                x_early(side, i).start()

    for side in range(2):
        @pl.when(jnp.logical_not(receives("gx", side)))
        def _():
            def clear(y, carry):
                hx[side, :, y] = jnp.zeros((2, CZ, NV), BF16)
                return carry
            lax.fori_loop(0, CY, clear, 0)

        @pl.when(jnp.logical_not(receives("gy", side)))
        def _():
            hy[side] = jnp.zeros((CX, 2, CZ, NV), BF16)

        @pl.when(jnp.logical_not(receives("gz", side)))
        def _():
            def clear(y, carry):
                hz[y, side] = jnp.zeros((2 * CX, NV), BF16)
                return carry
            lax.fori_loop(0, CY, clear, 0)

    eye[...] = jnp.where(iota((NV, NV), 0) == iota((NV, NV), 1), 1.0, 0.0).astype(BF16)

    r, c = iota((CELLS, CELLS), 0), iota((CELLS, CELLS), 1)
    same_x, same_z = (r >> 5) == (c >> 5), (r & 31) == (c & 31)
    along_z = jnp.where(same_x, tap(jnp.abs((r & 31) - (c & 31))), 0.0)
    along_x = jnp.where(same_z, tap(jnp.abs((r >> 5) - (c >> 5))), 0.0)
    at[...] = (along_x + along_z - jnp.where(r == c, 90.0, 0.0)).astype(BF16)

    r, c = iota((NV, CELLS), 0), iota((NV, CELLS), 1)
    k, x = (r >> 5) & 1, c >> 5
    dist = jnp.where(r < 64, x + 2 - k, CX + k - x)
    bt[...] = jnp.where((r & 31) == (c & 31), tap(dist), 0.0).astype(BF16)

    r, c = iota((2 * CELLS, NV), 0), iota((2 * CELLS, NV), 1)
    k, x = (c >> 5) & 1, (r >> 5) & 7
    dist = jnp.where(c < 64, CX + k - x, x + 2 - k)
    keep = ((r & 31) == (c & 31)) & ((r < CELLS) == (c < 64))
    bg[...] = jnp.where(keep, tap(dist), 0.0).astype(BF16)

    for j in range(4):
        r, c = iota((NV, CELLS), 0), iota((NV, CELLS), 1)
        k, z = r & 1, c & 31
        dist = jnp.where(((r >> 4) & 1) == 0, z + 2 - k, CZ + k - z)
        keep = ((r >> 5) == j) & (((r >> 1) & 7) == (c >> 5))
        ez[j] = jnp.where(keep, tap(dist), 0.0).astype(BF16)

    r, c = iota((32, CELLS), 0), iota((32, CELLS), 1)
    target = jnp.where(r < 16, CZ - 2, 0) + (r & 1)
    pz[...] = jnp.where(
        (((r >> 1) & 7) == (c >> 5)) & ((c & 31) == target), 1.0, 0.0
    ).astype(BF16)

    c_in[...] = jnp.zeros_like(c_in)
    h_in[...] = jnp.zeros_like(h_in)

    def add_to(total, value):
        rows = NV // nz
        total[...] += value.reshape(nz, rows, NV)

    def turn(i, carry):
        part = None
        for j in range(4):
            y = i * 4 + j
            block = u_v[:, y].reshape(CELLS, NV)
            turned = dot_nt(eye[...], block).astype(BF16)
            ut[y + 2] = turned
            zs[y] = dot_nn(pz[...], block).astype(BF16).reshape(2, 2 * CX, NV)
            term = dot_nn(turned, block)
            part = term if part is None else part + term
        add_to(c_in, part)
        return carry

    for i in range(LOADS):
        loads[i].wait()
        lax.fori_loop(i * per // 4, (i + 1) * per // 4, turn, 0)
        if (i + 1) % (LOADS // ZPIECES) == 0:
            for side in range(2):
                @pl.when(sends("gz", side))
                def _():
                    z_copy(side, i // (LOADS // ZPIECES)).start()

    def exchange(stage, axis, source, target):
        for off in range(1, size[axis]):
            peer = lax.rem(me[axis] + off, size[axis])
            send(source(peer), target, ar_send.at[stage], ar_recv.at[stage], axis, peer).start()

    def finish(stage, axis, like):
        whole = like.at[pl.ds(0, size[axis] - 1)]
        pltpu.make_async_copy(whole, whole, ar_recv.at[stage]).wait()
        pltpu.make_async_copy(whole, whole, ar_send.at[stage]).wait()

    def total(ref, count):
        out = ref[0]
        for i in range(1, count):
            out = out + ref[i]
        return out

    def stage0(base, source, z):
        exchange(base, "gz", lambda peer: source.at[peer], z.at[gz])
        z[gz] = source[gz]

    def stage1(base, z, y):
        finish(base, "gz", z)
        y[gy] = total(z, nz)
        exchange(base + 1, "gy", lambda peer: y.at[gy], y.at[gy])

    def stage2(base, y, x):
        finish(base + 1, "gy", y)
        x[gx] = total(y, ny)
        exchange(base + 2, "gx", lambda peer: x.at[gx], x.at[gx])

    def stage3(base, x, out):
        finish(base + 2, "gx", x)
        out[gz] = total(x, nx)
        exchange(base + 3, "gz", lambda peer: out.at[gz], out.at[gz])

    stage0(0, c_in, c_z)

    pot_load.wait()
    pott[...] = potv[...].reshape(CELLS, CY).T

    for side in range(2):
        @pl.when(receives("gy", side))
        def _():
            y_copy(side).wait_recv()
        for k in range(2):
            ut[(0 if side == 0 else CY + 2) + k] = dot_nt(
                eye[...], hy[side, :, k].reshape(CELLS, NV)
            ).astype(BF16)

    def apply(i, carry):
        halo = dot_nt(eye[...], hz[pl.ds(i * 4, 4)].reshape(NV, NV)).astype(BF16)
        part = None
        for j in range(4):
            y = i * 4 + j
            own = ut[y + 2]
            acc = dot_nn(own, at[...]) + dot_nn(halo, ez[j])
            near = ut[y + 1].astype(F32) + ut[y + 3].astype(F32)
            far = ut[y].astype(F32) + ut[y + 4].astype(F32)
            acc = acc + (16.0 * near - far)
            value = acc * (-1.0 / 24.0) + pott[pl.ds(y, 1), :] * own.astype(F32)
            appl[y] = value
            term = dot_nt(own, value.astype(BF16))
            part = term if part is None else part + term
        add_to(h_in, part)
        return carry

    groups = CY // ZPIECES // 4
    for i in range(ZPIECES):
        for side in range(2):
            @pl.when(receives("gz", side))
            def _():
                z_copy(side, i).wait_recv()
        lax.fori_loop(i * groups, (i + 1) * groups, apply, 0)
        if i == 0:
            stage1(0, c_z, c_y)
    stage2(0, c_y, c_x)

    def cross(i, carry):
        for j in range(2):
            p = i * 2 + j
            pair = jnp.concatenate([ut[p + 2], ut[p + 2 + HALF]], axis=1)
            xc[p] = (dot_nn(pair, bg[...]) * (-1.0 / 12.0)).astype(BF16)
        return carry

    lax.fori_loop(0, HALF // 2, cross, 0)
    stage3(0, c_x, c_out)

    for i in range(PIECES):
        for side in range(2):
            @pl.when(receives("gx", side))
            def _():
                x_early(side, i).wait_recv()
        part = None
        for j in range(early_n):
            p = i * early_n + j
            layers = jnp.concatenate(
                [hx[1, :, p].reshape(2 * CZ, NV), hx[0, :, p + HALF].reshape(2 * CZ, NV)], axis=0
            )
            term = dot_nn(xc[p], layers)
            part = term if part is None else part + term
        add_to(h_in, part)

    stage0(4, h_in, h_z)
    for i in range(LATE):
        for side in range(2):
            @pl.when(sends("gx", side))
            def _():
                x_late(side, i).start()

    finish(3, "gz", c_out)
    mat[...] = c_out[...].reshape(NV, NV) * (1.0 / ncell)

    def eliminate(b, carry):
        whole = mat[...]
        panel = mat[pl.ds(pl.multiple_of(b * 8, 8), 8), :]
        row_of, lane_of = iota((NV, NV), 0), iota((NV, NV), 1)
        prow, plane = iota((8, NV), 0), iota((8, NV), 1)
        for s in range(8):
            pivot_row = panel[s : s + 1, :]
            scale = 1.0 / panel[s : s + 1, s : s + 1]
            scaled = jnp.where(plane[:1] == s, scale, pivot_row * scale)
            below = row_of > b * 8 + s
            factor = jnp.where(below, jnp.broadcast_to(whole[:, s : s + 1], (NV, NV)), 0.0)
            whole = jnp.where(below & (lane_of == s), 0.0, whole) - factor * scaled
            if s < 7:
                below = prow > s
                factor = jnp.where(below, jnp.broadcast_to(panel[:, s : s + 1], (8, NV)), 0.0)
                panel = jnp.where(below & (plane == s), 0.0, panel) - factor * scaled
        mat[...] = pltpu.roll(whole, NV - 8, 1)
        return carry

    lax.fori_loop(0, 5, eliminate, 0)
    stage1(4, h_z, h_y)
    lax.fori_loop(5, 10, eliminate, 0)
    stage2(4, h_y, h_x)
    lax.fori_loop(10, 16, eliminate, 0)
    stage3(4, h_x, h_out)

    row_of, lane_of = iota((NV, NV), 0), iota((NV, NV), 1)
    one = jnp.where(row_of == lane_of, 1.0, 0.0)
    done = mat[...]
    diag = jnp.sum(done * one, axis=1, keepdims=True)
    lower = jnp.where(row_of > lane_of, done, one * 1.0) * lax.rsqrt(diag)
    lower = jnp.where(row_of >= lane_of, lower, 0.0)
    linv[...] = lower
    linvt[...] = lower.T

    def widen(i, carry):
        for j in range(2):
            y = i * 2 + j
            halo = dot_nt(eye[...], hx[:, :, y].reshape(NV, NV)).astype(BF16)
            appl[y] += dot_nn(halo, bt[...]) * (-1.0 / 24.0)
        return carry

    for i in range(LATE):
        for side in range(2):
            @pl.when(receives("gx", side))
            def _():
                x_late(side, i).wait_recv()
    lax.fori_loop(0, CY // 2, widen, 0)

    finish(7, "gz", h_out)
    lower = linv[...]
    hamil = h_out[...].reshape(NV, NV) * (1.0 / ncell)
    reduced = exact_nt(exact(lower, hamil), lower)
    reduced = 0.5 * (reduced + reduced.T)
    shifted = reduced - one * (jnp.sum(reduced * one) / NV)
    sign = shifted * lax.rsqrt(jnp.full((1, 1), jnp.sum(shifted * shifted) + 1e-06, F32))
    for step in range(FILTER_STEPS):
        square = exact(sign, sign)
        sign = 1.5 * sign - 0.5 * exact(square, sign)
    rot = exact(linvt[...], exact(0.5 * (one - sign), lower))
    rot = (0.5 * (rot + rot.T)).astype(BF16)

    def densities(i, carry):
        for j in range(2):
            y = i * 2 + j
            own = ut[y + 2]
            mixed = dot_nn(rot, own)
            rows_d[pl.ds(y, 1), :] = jnp.sum(own.astype(F32) * mixed, axis=0, keepdims=True)
            rows_e[pl.ds(y, 1), :] = jnp.sum(appl[y] * mixed, axis=0, keepdims=True)
        return carry

    lax.fori_loop(0, CY // 2, densities, 0)
    dens_out[...] = (rows_d[...].T * (1.0 / NB)).reshape(CX, CZ, CY)
    en_out[...] = (rows_e[...].T * (1.0 / NB)).reshape(CX, CZ, CY)

    for side in range(2):
        @pl.when(sends("gx", side))
        def _():
            for i in range(PIECES):
                x_early(side, i).wait_send()
            for i in range(LATE):
                x_late(side, i).wait_send()

        @pl.when(sends("gy", side))
        def _():
            y_copy(side).wait_send()

        @pl.when(sends("gz", side))
        def _():
            for i in range(ZPIECES):
                z_copy(side, i).wait_send()


def body(subspace, potential):
    sizes = tuple(lax.axis_size(name) for name in AXES)
    nx, ny, nz = sizes
    rows = NV // nz
    vm, dma = pltpu.VMEM, pltpu.SemaphoreType.DMA
    any_space = pl.BlockSpec(memory_space=pl.ANY)
    whole = pl.BlockSpec(memory_space=pltpu.VMEM)
    out = jax.ShapeDtypeStruct((CX, CZ, CY), F32)
    reduce_set = [
        vm((nz, rows, NV), F32), vm((nz, rows, NV), F32), vm((ny, rows, NV), F32),
        vm((nx, rows, NV), F32), vm((nz, rows, NV), F32),
    ]
    density, energy = pl.pallas_call(
        functools.partial(kernel, sizes),
        out_shape=(out, out),
        in_specs=[any_space, any_space],
        out_specs=(whole, whole),
        scratch_shapes=[
            vm((CX, CY, CZ, NV), BF16),
            vm((CY + 4, NV, CELLS), BF16),
            vm((CY, NV, CELLS), F32),
            vm((2, 2, CY, CZ, NV), BF16),
            vm((2, CX, 2, CZ, NV), BF16),
            vm((CY, 2, 2 * CX, NV), BF16),
            vm((CY, 2, 2 * CX, NV), BF16),
            vm((HALF, NV, NV), BF16),
            vm((CX, CZ, CY), F32),
            vm((CY, CELLS), F32),
            vm((CELLS, CELLS), BF16),
            vm((4, NV, CELLS), BF16),
            vm((NV, CELLS), BF16),
            vm((2 * CELLS, NV), BF16),
            vm((32, CELLS), BF16),
            vm((NV, NV), BF16),
            *reduce_set,
            *reduce_set,
            vm((NV, NV), F32),
            vm((NV, NV), F32),
            vm((NV, NV), F32),
            vm((CY, CELLS), F32),
            vm((CY, CELLS), F32),
            dma((LOADS + 1,)),
            dma((2, PIECES + LATE)),
            dma((2, PIECES + LATE)),
            dma((2,)),
            dma((2,)),
            dma((2, ZPIECES)),
            dma((2, ZPIECES)),
            dma((8,)),
            dma((8,)),
        ],
        compiler_params=pltpu.CompilerParams(
            collective_id=0, has_side_effects=True, vmem_limit_bytes=48 * 1024 * 1024
        ),
    )(subspace, jnp.transpose(potential, (0, 2, 1)))
    return jnp.transpose(density, (0, 2, 1)), jnp.transpose(energy, (0, 2, 1))


def solution(mesh):
    return jax.shard_map(
        body,
        mesh=mesh,
        in_specs=(P("gx", "gy", "gz", None), P("gx", "gy", "gz")),
        out_specs=(P("gx", "gy", "gz"), P("gx", "gy", "gz")),
        check_vma=False,
    )
```

time: 383 us -> 76 us (0.20)
  waiting for transfers between devices: 255 us -> 0 us
  Pallas kernels: 0 us -> 71.1 us
  other arithmetic: 59.5 us -> 0 us
  local copies, waits for them, and re-layouts: 24.4 us -> 4.1 us
  starting transfers between devices: 18.3 us -> 0 us
  between operations: 15.8 us -> 0.65 us
  matrix products: 9.58 us -> 0 us
    psum x1 -> x0, waiting for transfers between devices: 233 us -> none  [body(): correlation, hamil = lax.psum((local_over, local_hamil), ('gx', 'gy', 'gz'))]
    pallas_call x0 -> x1, Pallas kernels: none -> 71.1 us  [body(): pl.pallas_call(functools.partial(kernel, sizes), out_shape=(out, out), in...]
    convert_element_type x2 -> x0, other arithmetic: 26.8 us -> none  [the longest x1 22.5 us: body(): (-0.5 * laplace + potential[..., None] * subspace.astype(jnp.float32)).as...]
    another operation x5 -> x0, other arithmetic: 22.9 us -> none  [the longest x3 12.4 us: make_projector(): factor = jnp.linalg.cholesky(correlation)]
    ppermute x6 -> x0, waiting for transfers between devices: 21.5 us -> none  [the longest x3 15.1 us: with_halo(): lax.ppermute(lax.slice_in_dim(block, block.shape[dim] - width, None, axis...]
    ppermute x6 -> x0, starting transfers between devices: 18.3 us -> none  [the longest x3 13.8 us: with_halo(): lax.ppermute(lax.slice_in_dim(block, block.shape[dim] - width, None, axis...]
    dot_general x19 -> x0, matrix products: 7.7 us -> none  [the longest x1 1.73 us: body(): lax.dot_general(flat, applied_flat, contract, preferred_element_type=jnp....]
    convert_element_type x1 -> x0, local copies, waits for them, and re-layouts: 6.64 us -> none  [body(): energy = jnp.sum(applied_flat.astype(jnp.float32) * mixed, axis=1) / NB]
  transfers between devices with their start and end apart: 7 -> 0, of which waited for: 6 -> 0; matrix products, arithmetic and copies ran while one was open for 5% -> 0% of each run, Pallas kernels for 0% -> 0%
where the time goes in v2:
time: 76 us; the launch traced here: 75.9 us
  Pallas kernels  71.1 us (94%)
  local copies, waits for them, and re-layouts  4.1 us (5%)
    pallas_call x1, Pallas kernels, body(): pl.pallas_call(functools.partial(kernel, sizes), out_shape=(out, out), in...  71.1 us
    unnamed x6, local copies, waits for them, and re-layouts  4.1 us

profile of v2, /device:TPU:1, one launch (start us, length us, event | category | flops | bytes accessed | tf_op | source)
XLA Modules:
  0.0 75.9 jit_solution(11657679431214656282)
XLA Ops:
  0.6 0.0 copy-start
  0.6 1.9 %copy-done = bf16[8,48,32,128]{3,2,1,0:T(8,128)(2,1)S(1)} copy-done((bf16[8,48,32,128]{3,2,1,0:T(8,128)(2,1)S(1)}, bf16[8,48,32,128]{3,2,1,0:T(8,128)(2,1)}, u32[]{:S(2)}) %copy-start) | copy-done | bytes 3145752
  2.5 0.0 copy-start.1
  2.5 0.9 %copy-done.1 = f32[8,48,32]{1,2,0:T(8,128)S(1)} copy-done((f32[8,48,32]{1,2,0:T(8,128)S(1)}, f32[8,48,32]{1,2,0:T(8,128)}, u32[]{:S(2)}) %copy-start.1) | copy-done | bytes 49176
  3.4 71.1 %shard_map.41 = (f32[8,32,48]{2,1,0:T(8,128)S(1)}, f32[8,32,48]{2,1,0:T(8,128)S(1)}) custom-call(bf16[8,48,32,128]{3,2,1,0:T(8,128)(2,1)S(1)} %copy-done, f32[8,32,48]{2,1,0:T(8,128)S(1)} %bitcast.3), custom_call_target="tpu_custom_call" | custom-call | tf_op jit(solution)/shard_map/pallas_call | solution.py:435
  74.5 0.7 copy.6
  75.2 0.7 copy.7
Async XLA Ops:
  0.6 1.9 %copy-start = (bf16[8,48,32,128]{3,2,1,0:T(8,128)(2,1)S(1)}, bf16[8,48,32,128]{3,2,1,0:T(8,128)(2,1)}, u32[]{:S(2)}) copy-start(bf16[8,48,32,128]{3,2,1,0:T(8,128)(2,1)} %u_hbm.1) | copy-start | bytes 9437188
  2.5 0.9 %copy-start.1 = (f32[8,48,32]{1,2,0:T(8,128)S(1)}, f32[8,48,32]{1,2,0:T(8,128)}, u32[]{:S(2)}) copy-start(f32[8,48,32]{1,2,0:T(8,128)} %param.3) | copy-start | bytes 147460

commit v3 on v2

--- a/solution.py
+++ b/solution.py
@@ -20,6 +20,7 @@
 PIECES = 4
 LATE = 2
 ZPIECES = 2
+STACK = 8
 
 
 def place(axis, index):
@@ -53,9 +54,9 @@
 
 
 def kernel(
-    sizes, u_hbm, pot_hbm, dens_out, en_out,
-    u_v, ut, appl, hx, hy, hz, zs, xc, potv, pott, at, ez, bt, bg, pz, eye,
-    c_in, c_z, c_y, c_x, c_out, h_in, h_z, h_y, h_x, h_out, mat, linv, linvt, rows_d, rows_e,
+    sizes, u_hbm, pot_hbm, rows_d, rows_e,
+    u_v, ut, appl, hx, hy, hz, zs, xc, potv, pott, at, ez, bt, bg, pz,
+    c_in, c_z, c_y, c_x, c_out, h_in, h_z, h_y, h_x, h_out, mat, linv, linvt,
     load_sem, x_send, x_recv, y_send, y_recv, z_send, z_recv, ar_send, ar_recv,
 ):
     size = dict(zip(AXES, sizes))
@@ -78,7 +79,6 @@
         for off in range(1, size[axis]):
             peer = lax.rem(me[axis] + off, size[axis])
             pl.semaphore_signal(barrier, inc=1, device_id=place(axis, peer), device_id_type=MESH)
-    pl.semaphore_wait(barrier, nx + ny + nz - 3)
 
     def send(src, dst, ssem, rsem, axis, peer):
         return pltpu.make_async_remote_copy(
@@ -125,17 +125,6 @@
         return me[axis] > 0 if side == 0 else me[axis] < size[axis] - 1
 
     for side in range(2):
-        @pl.when(sends("gy", side))
-        def _():
-            y_copy(side).start()
-
-    for i in range(PIECES):
-        for side in range(2):
-            @pl.when(sends("gx", side))
-            def _():
-                x_early(side, i).start()
-
-    for side in range(2):
         @pl.when(jnp.logical_not(receives("gx", side)))
         def _():
             def clear(y, carry):
@@ -153,8 +142,6 @@
                 hz[y, side] = jnp.zeros((2 * CX, NV), BF16)
                 return carry
             lax.fori_loop(0, CY, clear, 0)
-
-    eye[...] = jnp.where(iota((NV, NV), 0) == iota((NV, NV), 1), 1.0, 0.0).astype(BF16)
 
     r, c = iota((CELLS, CELLS), 0), iota((CELLS, CELLS), 1)
     same_x, same_z = (r >> 5) == (c >> 5), (r & 31) == (c & 31)
@@ -171,20 +158,15 @@
     k, x = (c >> 5) & 1, (r >> 5) & 7
     dist = jnp.where(c < 64, CX + k - x, x + 2 - k)
     keep = ((r & 31) == (c & 31)) & ((r < CELLS) == (c < 64))
-    bg[...] = jnp.where(keep, tap(dist), 0.0).astype(BF16)
-
-    for j in range(4):
-        r, c = iota((NV, CELLS), 0), iota((NV, CELLS), 1)
-        k, z = r & 1, c & 31
-        dist = jnp.where(((r >> 4) & 1) == 0, z + 2 - k, CZ + k - z)
-        keep = ((r >> 5) == j) & (((r >> 1) & 7) == (c >> 5))
-        ez[j] = jnp.where(keep, tap(dist), 0.0).astype(BF16)
-
-    r, c = iota((32, CELLS), 0), iota((32, CELLS), 1)
-    target = jnp.where(r < 16, CZ - 2, 0) + (r & 1)
-    pz[...] = jnp.where(
-        (((r >> 1) & 7) == (c >> 5)) & ((c & 31) == target), 1.0, 0.0
-    ).astype(BF16)
+    bg[...] = jnp.where(keep, 2.0 * tap(dist), 0.0).astype(BF16)
+
+    r, c = iota((4 * CX, CELLS), 0), iota((4 * CX, CELLS), 1)
+    k, z = r & 1, c & 31
+    dist = jnp.where(r < 16, z + 2 - k, CZ + k - z)
+    ez[...] = jnp.where(((r >> 1) & 7) == (c >> 5), tap(dist), 0.0).astype(BF16)
+
+    target = jnp.where(r < 16, CZ - 2, 0) + k
+    pz[...] = jnp.where((((r >> 1) & 7) == (c >> 5)) & (z == target), 1.0, 0.0).astype(BF16)
 
     c_in[...] = jnp.zeros_like(c_in)
     h_in[...] = jnp.zeros_like(h_in)
@@ -198,17 +180,28 @@
         for j in range(4):
             y = i * 4 + j
             block = u_v[:, y].reshape(CELLS, NV)
-            turned = dot_nt(eye[...], block).astype(BF16)
+            turned = block.T
             ut[y + 2] = turned
-            zs[y] = dot_nn(pz[...], block).astype(BF16).reshape(2, 2 * CX, NV)
-            term = dot_nn(turned, block)
-            part = term if part is None else part + term
+            both = dot_nn(jnp.concatenate([turned, pz[...]], axis=0), block)
+            zs[y] = both[NV:].astype(BF16).reshape(2, 2 * CX, NV)
+            part = both[:NV] if part is None else part + both[:NV]
         add_to(c_in, part)
         return carry
 
     for i in range(LOADS):
         loads[i].wait()
         lax.fori_loop(i * per // 4, (i + 1) * per // 4, turn, 0)
+        if i == 0:
+            pl.semaphore_wait(barrier, nx + ny + nz - 3)
+            for side in range(2):
+                @pl.when(sends("gy", side))
+                def _():
+                    y_copy(side).start()
+            for n in range(PIECES):
+                for side in range(2):
+                    @pl.when(sends("gx", side))
+                    def _():
+                        x_early(side, n).start()
         if (i + 1) % (LOADS // ZPIECES) == 0:
             for side in range(2):
                 @pl.when(sends("gz", side))
@@ -253,35 +246,37 @@
     stage0(0, c_in, c_z)
 
     pot_load.wait()
-    pott[...] = potv[...].reshape(CELLS, CY).T
+    pott[...] = potv[...].reshape(CELLS, CY).T * -24.0
 
     for side in range(2):
         @pl.when(receives("gy", side))
         def _():
             y_copy(side).wait_recv()
         for k in range(2):
-            ut[(0 if side == 0 else CY + 2) + k] = dot_nt(
-                eye[...], hy[side, :, k].reshape(CELLS, NV)
-            ).astype(BF16)
+            ut[(0 if side == 0 else CY + 2) + k] = hy[side, :, k].reshape(CELLS, NV).T
 
     def apply(i, carry):
-        halo = dot_nt(eye[...], hz[pl.ds(i * 4, 4)].reshape(NV, NV)).astype(BF16)
+        first = i * STACK
+        halo = jnp.concatenate(
+            [hz[first + j].reshape(4 * CX, NV).T for j in range(STACK)], axis=0
+        )
+        acc = dot_nn(ut[pl.ds(first + 2, STACK)].reshape(STACK * NV, CELLS), at[...])
+        acc = acc + dot_nn(halo, ez[...])
         part = None
-        for j in range(4):
-            y = i * 4 + j
+        for j in range(STACK):
+            y = first + j
             own = ut[y + 2]
-            acc = dot_nn(own, at[...]) + dot_nn(halo, ez[j])
             near = ut[y + 1].astype(F32) + ut[y + 3].astype(F32)
             far = ut[y].astype(F32) + ut[y + 4].astype(F32)
-            acc = acc + (16.0 * near - far)
-            value = acc * (-1.0 / 24.0) + pott[pl.ds(y, 1), :] * own.astype(F32)
+            value = acc[j * NV : (j + 1) * NV] + (16.0 * near - far)
+            value = value + pott[pl.ds(y, 1), :] * own.astype(F32)
             appl[y] = value
             term = dot_nt(own, value.astype(BF16))
             part = term if part is None else part + term
         add_to(h_in, part)
         return carry
 
-    groups = CY // ZPIECES // 4
+    groups = CY // ZPIECES // STACK
     for i in range(ZPIECES):
         for side in range(2):
             @pl.when(receives("gz", side))
@@ -293,13 +288,14 @@
     stage2(0, c_y, c_x)
 
     def cross(i, carry):
-        for j in range(2):
-            p = i * 2 + j
-            pair = jnp.concatenate([ut[p + 2], ut[p + 2 + HALF]], axis=1)
-            xc[p] = (dot_nn(pair, bg[...]) * (-1.0 / 12.0)).astype(BF16)
+        span = pl.ds(i * STACK, STACK)
+        high = ut[pl.ds(i * STACK + 2, STACK)].reshape(STACK * NV, CELLS)
+        low = ut[pl.ds(i * STACK + 2 + HALF, STACK)].reshape(STACK * NV, CELLS)
+        both = dot_nn(high, bg[:CELLS]) + dot_nn(low, bg[CELLS:])
+        xc[span] = both.astype(BF16).reshape(STACK, NV, NV)
         return carry
 
-    lax.fori_loop(0, HALF // 2, cross, 0)
+    lax.fori_loop(0, HALF // STACK, cross, 0)
     stage3(0, c_x, c_out)
 
     for i in range(PIECES):
@@ -327,23 +323,41 @@
     finish(3, "gz", c_out)
     mat[...] = c_out[...].reshape(NV, NV) * (1.0 / ncell)
 
+    prow, plane = iota((8, NV), 0), iota((8, NV), 1)
+    outside = iota((NV, NV), 1) >= 8
+
+    def spread(x, s):
+        return jnp.broadcast_to(x[s : s + 1, :], (8, NV))
+
+    def split(x):
+        a = x.astype(BF16).astype(F32)
+        b = (x - a).astype(BF16).astype(F32)
+        return a, b, x - a - b
+
     def eliminate(b, carry):
-        whole = mat[...]
-        panel = mat[pl.ds(pl.multiple_of(b * 8, 8), 8), :]
-        row_of, lane_of = iota((NV, NV), 0), iota((NV, NV), 1)
-        prow, plane = iota((8, NV), 0), iota((8, NV), 1)
+        panel = mat[0:8, :]
+        column = [jnp.broadcast_to(panel[:, s : s + 1], (8, NV)) for s in range(8)]
+        inverse = jnp.zeros((8, NV), F32)
         for s in range(8):
-            pivot_row = panel[s : s + 1, :]
-            scale = 1.0 / panel[s : s + 1, s : s + 1]
-            scaled = jnp.where(plane[:1] == s, scale, pivot_row * scale)
-            below = row_of > b * 8 + s
-            factor = jnp.where(below, jnp.broadcast_to(whole[:, s : s + 1], (NV, NV)), 0.0)
-            whole = jnp.where(below & (lane_of == s), 0.0, whole) - factor * scaled
-            if s < 7:
-                below = prow > s
-                factor = jnp.where(below, jnp.broadcast_to(panel[:, s : s + 1], (8, NV)), 0.0)
-                panel = jnp.where(below & (plane == s), 0.0, panel) - factor * scaled
-        mat[...] = pltpu.roll(whole, NV - 8, 1)
+            below = prow > s
+            scale = 1.0 / spread(column[s], s)
+            factor = jnp.where(below, column[s] * scale, 0.0)
+            inverse = jnp.where(prow == s, scale, inverse)
+            row = jnp.where(plane == s, 1.0, spread(panel, s))
+            panel = jnp.where(below & (plane == s), 0.0, panel) - factor * row
+            for t in range(s + 1, 8):
+                column[t] = column[t] - factor * spread(column[t], s)
+        left = jnp.where((plane >= 8) & (plane < NV - 8 * b), panel, 0.0)
+        unit = jnp.where(plane < prow, panel, jnp.where(plane == prow, 1.0, 0.0))
+        right = jnp.where(plane < 8, unit, panel) * inverse
+        p0, p1, p2 = split(left)
+        q0, q1, q2 = split(right)
+        left = jnp.concatenate([p0, p0, p1, p0, p1, p2], axis=0).T.astype(BF16)
+        right = jnp.concatenate([q0, q1, q0, q2, q1, q0], axis=0).astype(BF16)
+        rest = jnp.where(outside, mat[...], 0.0) - dot_nn(left, right)
+        rest = pltpu.roll(rest, NV - 8, 1)
+        mat[0 : NV - 8, :] = rest[8:, :]
+        mat[NV - 8 :, :] = pltpu.roll(panel, NV - 8, 1)
         return carry
 
     lax.fori_loop(0, 5, eliminate, 0)
@@ -357,16 +371,16 @@
     one = jnp.where(row_of == lane_of, 1.0, 0.0)
     done = mat[...]
     diag = jnp.sum(done * one, axis=1, keepdims=True)
-    lower = jnp.where(row_of > lane_of, done, one * 1.0) * lax.rsqrt(diag)
-    lower = jnp.where(row_of >= lane_of, lower, 0.0)
+    lower = jnp.where(row_of > lane_of, done, one) * lax.rsqrt(diag)
     linv[...] = lower
     linvt[...] = lower.T
 
     def widen(i, carry):
-        for j in range(2):
-            y = i * 2 + j
-            halo = dot_nt(eye[...], hx[:, :, y].reshape(NV, NV)).astype(BF16)
-            appl[y] += dot_nn(halo, bt[...]) * (-1.0 / 24.0)
+        first = i * STACK
+        halo = jnp.concatenate(
+            [hx[:, :, first + j].reshape(NV, NV).T for j in range(STACK)], axis=0
+        )
+        appl[pl.ds(first, STACK)] += dot_nn(halo, bt[...]).reshape(STACK, NV, CELLS)
         return carry
 
     for i in range(LATE):
@@ -374,11 +388,11 @@
             @pl.when(receives("gx", side))
             def _():
                 x_late(side, i).wait_recv()
-    lax.fori_loop(0, CY // 2, widen, 0)
+    lax.fori_loop(0, CY // STACK, widen, 0)
 
     finish(7, "gz", h_out)
     lower = linv[...]
-    hamil = h_out[...].reshape(NV, NV) * (1.0 / ncell)
+    hamil = h_out[...].reshape(NV, NV) * (-1.0 / (24.0 * ncell))
     reduced = exact_nt(exact(lower, hamil), lower)
     reduced = 0.5 * (reduced + reduced.T)
     shifted = reduced - one * (jnp.sum(reduced * one) / NV)
@@ -390,17 +404,15 @@
     rot = (0.5 * (rot + rot.T)).astype(BF16)
 
     def densities(i, carry):
-        for j in range(2):
-            y = i * 2 + j
+        for j in range(STACK):
+            y = i * STACK + j
             own = ut[y + 2]
             mixed = dot_nn(rot, own)
             rows_d[pl.ds(y, 1), :] = jnp.sum(own.astype(F32) * mixed, axis=0, keepdims=True)
             rows_e[pl.ds(y, 1), :] = jnp.sum(appl[y] * mixed, axis=0, keepdims=True)
         return carry
 
-    lax.fori_loop(0, CY // 2, densities, 0)
-    dens_out[...] = (rows_d[...].T * (1.0 / NB)).reshape(CX, CZ, CY)
-    en_out[...] = (rows_e[...].T * (1.0 / NB)).reshape(CX, CZ, CY)
+    lax.fori_loop(0, CY // STACK, densities, 0)
 
     for side in range(2):
         @pl.when(sends("gx", side))
@@ -418,6 +430,11 @@
         def _():
             for i in range(ZPIECES):
                 z_copy(side, i).wait_send()
+
+
+def to_cells(rows_d, rows_e, density, energy):
+    density[...] = (rows_d[...].T * (1.0 / NB)).reshape(CX, CZ, CY)
+    energy[...] = (rows_e[...].T * (-1.0 / (24.0 * NB))).reshape(CX, CZ, CY)
 
 
 def body(subspace, potential):
@@ -425,16 +442,17 @@
     nx, ny, nz = sizes
     rows = NV // nz
     vm, dma = pltpu.VMEM, pltpu.SemaphoreType.DMA
-    any_space = pl.BlockSpec(memory_space=pl.ANY)
+    any_space = pl.BlockSpec(memory_space=pltpu.HBM)
     whole = pl.BlockSpec(memory_space=pltpu.VMEM)
+    rows_out = jax.ShapeDtypeStruct((CY, CELLS), F32)
     out = jax.ShapeDtypeStruct((CX, CZ, CY), F32)
     reduce_set = [
         vm((nz, rows, NV), F32), vm((nz, rows, NV), F32), vm((ny, rows, NV), F32),
         vm((nx, rows, NV), F32), vm((nz, rows, NV), F32),
     ]
-    density, energy = pl.pallas_call(
+    rows_d, rows_e = pl.pallas_call(
         functools.partial(kernel, sizes),
-        out_shape=(out, out),
+        out_shape=(rows_out, rows_out),
         in_specs=[any_space, any_space],
         out_specs=(whole, whole),
         scratch_shapes=[
@@ -449,18 +467,15 @@
             vm((CX, CZ, CY), F32),
             vm((CY, CELLS), F32),
             vm((CELLS, CELLS), BF16),
-            vm((4, NV, CELLS), BF16),
+            vm((4 * CX, CELLS), BF16),
             vm((NV, CELLS), BF16),
             vm((2 * CELLS, NV), BF16),
-            vm((32, CELLS), BF16),
-            vm((NV, NV), BF16),
+            vm((4 * CX, CELLS), BF16),
             *reduce_set,
             *reduce_set,
             vm((NV, NV), F32),
             vm((NV, NV), F32),
             vm((NV, NV), F32),
-            vm((CY, CELLS), F32),
-            vm((CY, CELLS), F32),
             dma((LOADS + 1,)),
             dma((2, PIECES + LATE)),
             dma((2, PIECES + LATE)),
@@ -472,9 +487,12 @@
             dma((8,)),
         ],
         compiler_params=pltpu.CompilerParams(
-            collective_id=0, has_side_effects=True, vmem_limit_bytes=48 * 1024 * 1024
+            collective_id=0, has_side_effects=True, vmem_limit_bytes=61 * 1024 * 1024
         ),
     )(subspace, jnp.transpose(potential, (0, 2, 1)))
+    density, energy = pl.pallas_call(
+        to_cells, out_shape=(out, out), in_specs=[whole, whole], out_specs=(whole, whole)
+    )(rows_d, rows_e)
     return jnp.transpose(density, (0, 2, 1)), jnp.transpose(energy, (0, 2, 1))
 
 

time: 76 us -> 54.1 us (0.71)
  Pallas kernels: 71.1 us -> 53.3 us
  local copies, waits for them, and re-layouts: 4.1 us -> 0 us
    pallas_call x1 -> x2, Pallas kernels: 71.1 us -> 53.3 us  [the longest x1 51.7 us: body(): pl.pallas_call(functools.partial(kernel, sizes), out_shape=(rows_out, row...]
    unnamed x6 -> x0, local copies, waits for them, and re-layouts: 4.1 us -> none
where the time goes in v3:
time: 54.1 us; the launch traced here: 54 us
  Pallas kernels  53.3 us (99%)
  between operations  0.64 us (1%)
    pallas_call x1, Pallas kernels, body(): pl.pallas_call(functools.partial(kernel, sizes), out_shape=(rows_out, row...  51.7 us
    pallas_call x1, Pallas kernels, body(): pl.pallas_call(to_cells, out_shape=(out, out), in_specs=[whole, whole], o...  1.62 us

profile of v3, /device:TPU:1, one launch (start us, length us, event | category | flops | bytes accessed | tf_op | source)
XLA Modules:
  0.0 54.0 jit_solution(2775606672866118905)
XLA Ops:
  0.6 51.7 %shard_map.41 = (f32[48,256]{1,0:T(8,128)}, f32[48,256]{1,0:T(8,128)}) custom-call(bf16[8,48,32,128]{3,2,1,0:T(8,128)(2,1)} %u_hbm.1, f32[8,32,48]{2,1,0:T(8,128)} %bitcast.3), custom_call_target="tpu_custom_call" | custom-call | tf_op jit(solution)/shard_map/pallas_call | solution.py:453
  52.4 1.6 %shard_map.42 = (f32[8,32,48]{2,1,0:T(8,128)}, f32[8,32,48]{2,1,0:T(8,128)}) custom-call(f32[48,256]{1,0:T(8,128)} %get-tuple-element.6.rows_d, f32[48,256]{1,0:T(8,128)} %get-tuple-element.7.rows_e), custom_call_target="tpu_custom_call" | custom-call | tf_op jit(solution)/shard_map/pallas_call | solution.py:493

commit v4 on v3

v4 whole, which is shorter than its diff:
```python
import functools

import jax
import jax.numpy as jnp
from jax import lax
from jax.experimental import pallas as pl
from jax.experimental.pallas import tpu as pltpu
from jax.sharding import PartitionSpec as P

NB = 64
FILTER_STEPS = 8
MESH = pl.DeviceIdType.MESH
AXES = ("gx", "gy", "gz")
F32, BF16 = jnp.float32, jnp.bfloat16

CX, CY, CZ, NV = 8, 48, 32, 128
CELLS = CX * CZ
HALF = CY // 2
LOADS = 2
PIECES = 4
LATE = 3
ZPIECES = 2
STACK = 16


def place(axis, index):
    return tuple(index if name == axis else lax.axis_index(name) for name in AXES)


def iota(shape, dim):
    return lax.broadcasted_iota(jnp.int32, shape, dim)


def tap(distance):
    return jnp.where(distance == 1, 16.0, 0.0) - jnp.where(distance == 2, 1.0, 0.0)


def dot_nn(a, b):
    return jnp.dot(a, b, preferred_element_type=F32)


def dot_nt(a, b):
    return lax.dot_general(a, b, (((1,), (1,)), ((), ())), preferred_element_type=F32)


def exact(a, b):
    return jnp.dot(a, b, precision=lax.Precision.HIGHEST, preferred_element_type=F32)


def three(a, b):
    a0, b0 = a.astype(BF16), b.astype(BF16)
    a1, b1 = (a - a0.astype(F32)).astype(BF16), (b - b0.astype(F32)).astype(BF16)
    return dot_nn(jnp.concatenate([a0, a0, a1], axis=1), jnp.concatenate([b0, b1, b0], axis=0))


def exact_nt(a, b):
    return lax.dot_general(
        a, b, (((1,), (1,)), ((), ())), precision=lax.Precision.HIGHEST, preferred_element_type=F32
    )


def kernel(
    sizes, u_hbm, pot_hbm, rows_d, rows_e,
    u_v, ut, appl, rounded, hx, hy, hz, zs, xc, potv, pott, at, ez, bt, bg, pz,
    total_c, c_in, c_part, c_x, c_out, total_h, h_in, h_part, h_x, h_out, mat, linv, linvt,
    load_sem, x_send, x_recv, y_send, y_recv, z_send, z_recv, ar_send, ar_recv,
):
    size = dict(zip(AXES, sizes))
    me = {name: lax.axis_index(name) for name in AXES}
    gx, gy, gz = me["gx"], me["gy"], me["gz"]
    nx, ny, nz = sizes
    ncell = float(nx * ny * nz * CX * CY * CZ)

    per = CY // LOADS
    loads = []
    for i in range(LOADS):
        span = pl.ds(i * per, per)
        loads.append(pltpu.make_async_copy(u_hbm.at[:, span], u_v.at[:, span], load_sem.at[i]))
        loads[-1].start()
    pot_load = pltpu.make_async_copy(pot_hbm, potv, load_sem.at[LOADS])
    pot_load.start()

    barrier = pltpu.get_barrier_semaphore()
    rows_of_x = [place("gx", lax.rem(gx + off, nx)) for off in range(1, nx)]
    plane = []
    for off in range(1, ny * nz):
        py, pz_at = lax.rem(gy + off // nz, ny), lax.rem(gz + off % nz, nz)
        plane.append((py * nz + pz_at, (gx, py, pz_at)))
    here = gy * nz + gz
    for peer in rows_of_x + [peer for _, peer in plane]:
        pl.semaphore_signal(barrier, inc=1, device_id=peer, device_id_type=MESH)

    def send(src, dst, ssem, rsem, axis, peer):
        return pltpu.make_async_remote_copy(
            src_ref=src, dst_ref=dst, send_sem=ssem, recv_sem=rsem,
            device_id=place(axis, peer), device_id_type=MESH,
        )

    def x_copy(side, start, count, slot):
        layers = pl.ds(CX - 2, 2) if side == 0 else pl.ds(0, 2)
        span = pl.ds(start, count)
        peer = lax.rem(gx + 1, nx) if side == 0 else lax.rem(gx + nx - 1, nx)
        return send(
            u_hbm.at[layers, span], hx.at[side, :, span],
            x_send.at[side, slot], x_recv.at[side, slot], "gx", peer,
        )

    early_n, late_n = HALF // PIECES, HALF // LATE

    def x_early(side, i):
        return x_copy(side, (HALF if side == 0 else 0) + i * early_n, early_n, i)

    def x_late(side, i):
        return x_copy(side, (0 if side == 0 else HALF) + i * late_n, late_n, PIECES + i)

    def y_copy(side):
        layers = pl.ds(CY - 2, 2) if side == 0 else pl.ds(0, 2)
        peer = lax.rem(gy + 1, ny) if side == 0 else lax.rem(gy + ny - 1, ny)
        return send(
            u_hbm.at[:, layers], hy.at[side], y_send.at[side], y_recv.at[side], "gy", peer
        )

    def z_copy(side, i):
        span = pl.ds(i * (CY // ZPIECES), CY // ZPIECES)
        peer = lax.rem(gz + 1, nz) if side == 0 else lax.rem(gz + nz - 1, nz)
        return send(
            zs.at[span, side], hz.at[span, side],
            z_send.at[side, i], z_recv.at[side, i], "gz", peer,
        )

    def sends(axis, side):
        return me[axis] < size[axis] - 1 if side == 0 else me[axis] > 0

    def receives(axis, side):
        return me[axis] > 0 if side == 0 else me[axis] < size[axis] - 1

    r, c = iota((CELLS, CELLS), 0), iota((CELLS, CELLS), 1)
    same_x, same_z = (r >> 5) == (c >> 5), (r & 31) == (c & 31)
    along_z = jnp.where(same_x, tap(jnp.abs((r & 31) - (c & 31))), 0.0)
    along_x = jnp.where(same_z, tap(jnp.abs((r >> 5) - (c >> 5))), 0.0)
    at[...] = (along_x + along_z - jnp.where(r == c, 90.0, 0.0)).astype(BF16)

    r, c = iota((NV, CELLS), 0), iota((NV, CELLS), 1)
    k, x = (r >> 5) & 1, c >> 5
    dist = jnp.where(r < 64, x + 2 - k, CX + k - x)
    bt[...] = jnp.where((r & 31) == (c & 31), tap(dist), 0.0).astype(BF16)

    r, c = iota((CELLS, NV), 0), iota((CELLS, NV), 1)
    k, x = (c >> 5) & 1, (r >> 5) & 3
    dist = jnp.where(c < 64, CX // 2 + k - x, x + 2 - k)
    keep = ((r & 31) == (c & 31)) & ((r < NV) == (c < 64))
    bg[...] = jnp.where(keep, 2.0 * tap(dist), 0.0).astype(BF16)

    r, c = iota((4 * CX, CELLS), 0), iota((4 * CX, CELLS), 1)
    k, z = r & 1, c & 31
    dist = jnp.where(r < 16, z + 2 - k, CZ + k - z)
    ez[...] = jnp.where(((r >> 1) & 7) == (c >> 5), tap(dist), 0.0).astype(BF16)

    total_c[...] = jnp.zeros_like(total_c)
    total_h[...] = jnp.zeros_like(total_h)

    r, c = iota((4 * CX, CELLS), 0), iota((4 * CX, CELLS), 1)
    target = jnp.where(r < 16, CZ - 2, 0) + (r & 1)
    keep = (((r >> 1) & 7) == (c >> 5)) & ((c & 31) == target)
    pz[...] = jnp.where(keep, 1.0, 0.0).astype(BF16)

    def turn(i, carry):
        part = None
        for j in range(per):
            y = i * per + j
            block = u_v[:, y].reshape(CELLS, NV)
            turned = block.T
            ut[y + 2] = turned
            both = dot_nn(jnp.concatenate([turned, pz[...]], axis=0), block)
            zs[y] = both[NV:].astype(BF16).reshape(2, 2 * CX, NV)
            part = both[:NV] if part is None else part + both[:NV]
        total_c[...] += part
        return carry

    for i in range(LOADS):
        loads[i].wait()
        lax.fori_loop(i, i + 1, turn, 0)
        if i == 0:
            pl.semaphore_wait(barrier, nx + ny * nz - 2)
            for n in range(PIECES - 1):
                for side in range(2):
                    @pl.when(sends("gx", side))
                    def _():
                        x_early(side, n).start()
            for side in range(2):
                @pl.when(sends("gz", side))
                def _():
                    z_copy(side, 0).start()

    slices = ny * nz
    thin = NV // slices

    def total(ref, count):
        parts = [ref[i] for i in range(count)]
        while len(parts) > 1:
            parts = [a + b for a, b in zip(parts[::2], parts[1::2])] + parts[len(parts) & ~1 :]
        return parts[0]

    def post(stage, source, target, peer):
        pltpu.make_async_remote_copy(
            src_ref=source, dst_ref=target, send_sem=ar_send.at[stage], recv_sem=ar_recv.at[stage],
            device_id=peer, device_id_type=MESH,
        ).start()

    def finish(stage, like, count):
        whole = like.at[pl.ds(0, count)]
        pltpu.make_async_copy(whole, whole, ar_recv.at[stage]).wait()
        pltpu.make_async_copy(whole, whole, ar_send.at[stage]).wait()

    def scatter(base, whole, source, part):
        for i in range(slices):
            source[i] = whole[i * thin : (i + 1) * thin, :]
        for there, peer in plane:
            post(base, source.at[there], part.at[here], peer)
        part[here] = source[here]

    def across(base, part, x):
        finish(base, part, slices - 1)
        x[gx] = total(part, slices)
        for peer in rows_of_x:
            post(base + 1, x.at[gx], x.at[gx], peer)

    def gather(base, x, out):
        finish(base + 1, x, nx - 1)
        out[here] = total(x, nx)
        for _, peer in plane:
            post(base + 2, out.at[here], out.at[here], peer)

    def gathered(base, out):
        finish(base + 2, out, slices - 1)
        return jnp.concatenate([out[i] for i in range(slices)], axis=0)

    scatter(0, total_c, c_in, c_part)
    for side in range(2):
        @pl.when(sends("gz", side))
        def _():
            z_copy(side, 1).start()

        @pl.when(sends("gy", side))
        def _():
            y_copy(side).start()

    for side in range(2):
        @pl.when(jnp.logical_not(receives("gx", side)))
        def _():
            def clear(y, carry):
                hx[side, :, y] = jnp.zeros((2, CZ, NV), BF16)
                return carry
            lax.fori_loop(0, CY, clear, 0)

        @pl.when(jnp.logical_not(receives("gy", side)))
        def _():
            hy[side] = jnp.zeros((CX, 2, CZ, NV), BF16)

        @pl.when(jnp.logical_not(receives("gz", side)))
        def _():
            def clear(y, carry):
                hz[y, side] = jnp.zeros((2 * CX, NV), BF16)
                return carry
            lax.fori_loop(0, CY, clear, 0)

    high = ut[2 : HALF + 2, :, NV:].reshape(HALF * NV, NV)
    low = ut[HALF + 2 : CY + 2, :, :NV].reshape(HALF * NV, NV)
    both = dot_nn(jnp.concatenate([high, low], axis=1), bg[...])
    xc[...] = both.astype(BF16).reshape(HALF, NV, NV)

    pot_load.wait()
    pott[...] = potv[...].reshape(CELLS, CY).T * -24.0
    ut[0:2] = jnp.zeros((2, NV, CELLS), BF16)
    ut[CY + 2 : CY + 4] = jnp.zeros((2, NV, CELLS), BF16)

    span = CY // ZPIECES

    def apply(first):
        halo = [hz[first + j].reshape(4 * CX, NV).T for j in range(span)]
        rows = jnp.concatenate(
            [ut[first + 2 : first + 2 + span].reshape(span * NV, CELLS), jnp.concatenate(halo, axis=0)],
            axis=1,
        )
        acc = dot_nn(rows, jnp.concatenate([at[...], ez[...]], axis=0))
        for strip in range(0, NV, 16):
            part = slice(strip, strip + 16)
            cell = [ut[first + j, part, :].astype(F32) for j in range(span + 4)]
            for j in range(span):
                y = first + j
                value = acc[j * NV + strip : j * NV + strip + 16]
                value = value + (16.0 * (cell[j + 1] + cell[j + 3]) - (cell[j] + cell[j + 4]))
                value = value + pott[y : y + 1, :] * cell[j + 2]
                appl[y, part, :] = value
                rounded[y, part, :] = value.astype(BF16)

    def product(cells):
        part = None
        for y in cells:
            term = dot_nt(ut[y + 2], rounded[y])
            part = term if part is None else part + term
        total_h[...] += part

    def z_arrived(i):
        for side in range(2):
            @pl.when(receives("gz", side))
            def _():
                z_copy(side, i).wait_recv()

    z_arrived(0)
    apply(0)
    across(0, c_part, c_x)
    for side in range(2):
        @pl.when(sends("gx", side))
        def _():
            x_early(side, PIECES - 1).start()
    z_arrived(1)
    apply(span)
    product(range(2, span))

    for side in range(2):
        @pl.when(receives("gy", side))
        def _():
            y_copy(side).wait_recv()
    for side, far, near in ((0, 0, 1), (1, CY - 1, CY - 2)):
        first = hy[side, :, 1 - side].reshape(CELLS, NV).T.astype(F32)
        second = hy[side, :, side].reshape(CELLS, NV).T.astype(F32)
        appl[far] += 16.0 * first - second
        appl[near] -= first
        rounded[far] = appl[far].astype(BF16)
        rounded[near] = appl[near].astype(BF16)
    product([0, 1, *range(span, CY)])


    for i in range(PIECES):
        for side in range(2):
            @pl.when(receives("gx", side))
            def _():
                x_early(side, i).wait_recv()
        part = None
        for j in range(early_n):
            p = i * early_n + j
            layers = jnp.concatenate(
                [hx[1, :, p].reshape(2 * CZ, NV), hx[0, :, p + HALF].reshape(2 * CZ, NV)], axis=0
            )
            term = dot_nn(xc[p], layers)
            part = term if part is None else part + term
        total_h[...] += part

    scatter(3, total_h, h_in, h_part)
    for side in range(2):
        @pl.when(sends("gx", side))
        def _():
            for i in range(LATE - 1):
                x_late(side, i).start()

    gather(0, c_x, c_out)

    def widen(late):
        for i in range(2):
            side = i if late else 1 - i
            halo = [hx[side, :, i * HALF + j].reshape(2 * CZ, NV).T for j in range(HALF)]
            taps = bt[side * 2 * CZ : (side + 1) * 2 * CZ, side * NV : (side + 1) * NV]
            more = dot_nn(jnp.concatenate(halo, axis=0), taps).reshape(HALF, NV, NV)
            appl[i * HALF : (i + 1) * HALF, :, side * NV : (side + 1) * NV] += more

    widen(False)
    across(3, h_part, h_x)

    mat[...] = gathered(0, c_out) * (1.0 / ncell)

    prow, lane = iota((8, NV), 0), iota((8, NV), 1)
    outside = iota((NV, NV), 1) >= 8

    def spread(x, s):
        return jnp.broadcast_to(x[s : s + 1, :], (8, NV))

    def split(x):
        a = x.astype(BF16).astype(F32)
        b = (x - a).astype(BF16).astype(F32)
        return a, b, x - a - b

    def eliminate(b, carry):
        panel = mat[0:8, :]
        column = [jnp.broadcast_to(panel[:, s : s + 1], (8, NV)) for s in range(8)]
        inverse = jnp.zeros((8, NV), F32)
        for s in range(8):
            below = prow > s
            scale = 1.0 / spread(column[s], s)
            factor = jnp.where(below, column[s] * scale, 0.0)
            inverse = jnp.where(prow == s, scale, inverse)
            row = jnp.where(lane == s, 1.0, spread(panel, s))
            panel = jnp.where(below & (lane == s), 0.0, panel) - factor * row
            for t in range(s + 1, 8):
                column[t] = column[t] - factor * spread(column[t], s)
        left = jnp.where((lane >= 8) & (lane < NV - 8 * b), panel, 0.0)
        unit = jnp.where(lane < prow, panel, jnp.where(lane == prow, 1.0, 0.0))
        right = jnp.where(lane < 8, unit, panel) * inverse
        p0, p1, p2 = split(left)
        q0, q1, q2 = split(right)
        left = jnp.concatenate([p0, p0, p1, p0, p1, p2], axis=0).T.astype(BF16)
        right = jnp.concatenate([q0, q1, q0, q2, q1, q0], axis=0).astype(BF16)
        rest = jnp.where(outside, mat[...], 0.0) - dot_nn(left, right)
        rest = pltpu.roll(rest, NV - 8, 1)
        mat[0 : NV - 8, :] = rest[8:, :]
        mat[NV - 8 :, :] = pltpu.roll(panel, NV - 8, 1)
        return carry

    lax.fori_loop(0, 9, eliminate, 0)
    gather(3, h_x, h_out)
    for side in range(2):
        @pl.when(sends("gx", side))
        def _():
            x_late(side, LATE - 1).start()
    lax.fori_loop(9, 16, eliminate, 0)

    row_of, lane_of = iota((NV, NV), 0), iota((NV, NV), 1)
    one = jnp.where(row_of == lane_of, 1.0, 0.0)
    done = mat[...]
    diag = jnp.sum(done * one, axis=1, keepdims=True)
    lower = jnp.where(row_of > lane_of, done, one) * lax.rsqrt(diag)
    linv[...] = lower
    linvt[...] = lower.T

    for i in range(LATE):
        for side in range(2):
            @pl.when(receives("gx", side))
            def _():
                x_late(side, i).wait_recv()
    widen(True)

    lower = linv[...]
    hamil = gathered(3, h_out) * (-1.0 / (24.0 * ncell))
    reduced = exact_nt(exact(lower, hamil), lower)
    reduced = 0.5 * (reduced + reduced.T)
    shifted = reduced - one * (jnp.sum(reduced * one) / NV)
    sign = shifted * lax.rsqrt(jnp.full((1, 1), jnp.sum(shifted * shifted) + 1e-06, F32))
    for step in range(FILTER_STEPS):
        square = three(sign, sign)
        sign = 1.5 * sign - 0.5 * three(square, sign)
    rot = exact(linvt[...], exact(0.5 * (one - sign), lower))
    rot = (0.5 * (rot + rot.T)).astype(BF16)

    def densities(i, carry):
        for j in range(STACK):
            y = i * STACK + j
            own = ut[y + 2]
            mixed = dot_nn(rot, own)
            rows_d[pl.ds(y, 1), :] = jnp.sum(own.astype(F32) * mixed, axis=0, keepdims=True)
            rows_e[pl.ds(y, 1), :] = jnp.sum(appl[y] * mixed, axis=0, keepdims=True)
        return carry

    lax.fori_loop(0, CY // STACK, densities, 0)

    for side in range(2):
        @pl.when(sends("gx", side))
        def _():
            for i in range(PIECES):
                x_early(side, i).wait_send()
            for i in range(LATE):
                x_late(side, i).wait_send()

        @pl.when(sends("gy", side))
        def _():
            y_copy(side).wait_send()

        @pl.when(sends("gz", side))
        def _():
            for i in range(ZPIECES):
                z_copy(side, i).wait_send()


def to_cells(rows_d, rows_e, density, energy):
    density[...] = (rows_d[...].T * (1.0 / NB)).reshape(CX, CZ, CY)
    energy[...] = (rows_e[...].T * (-1.0 / (24.0 * NB))).reshape(CX, CZ, CY)


def body(subspace, potential):
    sizes = tuple(lax.axis_size(name) for name in AXES)
    nx, ny, nz = sizes
    vm, dma = pltpu.VMEM, pltpu.SemaphoreType.DMA
    any_space = pl.BlockSpec(memory_space=pltpu.HBM)
    whole = pl.BlockSpec(memory_space=pltpu.VMEM)
    rows_out = jax.ShapeDtypeStruct((CY, CELLS), F32)
    out = jax.ShapeDtypeStruct((CX, CZ, CY), F32)
    slices = ny * nz
    thin = NV // slices
    reduce_set = [
        vm((NV, NV), F32),
        vm((slices, thin, NV), F32), vm((slices, thin, NV), F32),
        vm((nx, thin, NV), F32), vm((slices, thin, NV), F32),
    ]
    rows_d, rows_e = pl.pallas_call(
        functools.partial(kernel, sizes),
        out_shape=(rows_out, rows_out),
        in_specs=[any_space, any_space],
        out_specs=(whole, whole),
        scratch_shapes=[
            vm((CX, CY, CZ, NV), BF16),
            vm((CY + 4, NV, CELLS), BF16),
            vm((CY, NV, CELLS), F32),
            vm((CY, NV, CELLS), BF16),
            vm((2, 2, CY, CZ, NV), BF16),
            vm((2, CX, 2, CZ, NV), BF16),
            vm((CY, 2, 2 * CX, NV), BF16),
            vm((CY, 2, 2 * CX, NV), BF16),
            vm((HALF, NV, NV), BF16),
            vm((CX, CZ, CY), F32),
            vm((CY, CELLS), F32),
            vm((CELLS, CELLS), BF16),
            vm((4 * CX, CELLS), BF16),
            vm((NV, CELLS), BF16),
            vm((CELLS, NV), BF16),
            vm((4 * CX, CELLS), BF16),
            *reduce_set,
            *reduce_set,
            vm((NV, NV), F32),
            vm((NV, NV), F32),
            vm((NV, NV), F32),
            dma((LOADS + 1,)),
            dma((2, PIECES + LATE)),
            dma((2, PIECES + LATE)),
            dma((2,)),
            dma((2,)),
            dma((2, ZPIECES)),
            dma((2, ZPIECES)),
            dma((6,)),
            dma((6,)),
        ],
        compiler_params=pltpu.CompilerParams(
            collective_id=0, has_side_effects=True, vmem_limit_bytes=61 * 1024 * 1024
        ),
    )(subspace, jnp.transpose(potential, (0, 2, 1)))
    density, energy = pl.pallas_call(
        to_cells, out_shape=(out, out), in_specs=[whole, whole], out_specs=(whole, whole)
    )(rows_d, rows_e)
    return jnp.transpose(density, (0, 2, 1)), jnp.transpose(energy, (0, 2, 1))


def solution(mesh):
    return jax.shard_map(
        body,
        mesh=mesh,
        in_specs=(P("gx", "gy", "gz", None), P("gx", "gy", "gz")),
        out_specs=(P("gx", "gy", "gz"), P("gx", "gy", "gz")),
        check_vma=False,
    )
```

time: 54.1 us -> 46.2 us (0.85)
  Pallas kernels: 53.3 us -> 45.4 us
    pallas_call x1, Pallas kernels: 51.7 us -> 43.8 us  [body(): pl.pallas_call(functools.partial(kernel, sizes), out_shape=(rows_out, row...]
where the time goes in v4:
time: 46.2 us; the launch traced here: 46 us
  Pallas kernels  45.4 us (98%)
  between operations  0.64 us (1%)
    pallas_call x1, Pallas kernels, body(): pl.pallas_call(functools.partial(kernel, sizes), out_shape=(rows_out, row...  43.8 us
    pallas_call x1, Pallas kernels, body(): pl.pallas_call(to_cells, out_shape=(out, out), in_specs=[whole, whole], o...  1.62 us

profile of v4, /device:TPU:1, one launch (start us, length us, event | category | flops | bytes accessed | tf_op | source)
XLA Modules:
  0.0 46.0 jit_solution(16073287607320622710)
XLA Ops:
  0.6 43.8 %shard_map.41 = (f32[48,256]{1,0:T(8,128)}, f32[48,256]{1,0:T(8,128)}) custom-call(bf16[8,48,32,128]{3,2,1,0:T(8,128)(2,1)} %u_hbm.1, f32[8,32,48]{2,1,0:T(8,128)} %bitcast.3), custom_call_target="tpu_custom_call" | custom-call | tf_op jit(solution)/shard_map/pallas_call | solution.py:493
  44.4 1.6 %shard_map.42 = (f32[8,32,48]{2,1,0:T(8,128)}, f32[8,32,48]{2,1,0:T(8,128)}) custom-call(f32[48,256]{1,0:T(8,128)} %get-tuple-element.6.rows_d, f32[48,256]{1,0:T(8,128)} %get-tuple-element.7.rows_e), custom_call_target="tpu_custom_call" | custom-call | tf_op jit(solution)/shard_map/pallas_call | solution.py:534

commit v5 on v4

--- a/solution.py
+++ b/solution.py
@@ -18,7 +18,7 @@
 HALF = CY // 2
 LOADS = 2
 PIECES = 4
-LATE = 3
+LATE = 4
 ZPIECES = 2
 STACK = 16
 
@@ -180,17 +180,17 @@
     for i in range(LOADS):
         loads[i].wait()
         lax.fori_loop(i, i + 1, turn, 0)
-        if i == 0:
-            pl.semaphore_wait(barrier, nx + ny * nz - 2)
+
+    pl.semaphore_wait(barrier, nx + ny * nz - 2)
+    for side in range(2):
+        @pl.when(sends("gx", side))
+        def _():
             for n in range(PIECES - 1):
-                for side in range(2):
-                    @pl.when(sends("gx", side))
-                    def _():
-                        x_early(side, n).start()
-            for side in range(2):
-                @pl.when(sends("gz", side))
-                def _():
-                    z_copy(side, 0).start()
+                x_early(side, n).start()
+
+        @pl.when(sends("gz", side))
+        def _():
+            z_copy(side, 0).start()
 
     slices = ny * nz
     thin = NV // slices
@@ -319,6 +319,12 @@
     product(range(2, span))
 
     for side in range(2):
+        @pl.when(sends("gx", side))
+        def _():
+            for i in range(LATE - 1):
+                x_late(side, i).start()
+
+    for side in range(2):
         @pl.when(receives("gy", side))
         def _():
             y_copy(side).wait_recv()
@@ -348,11 +354,6 @@
         total_h[...] += part
 
     scatter(3, total_h, h_in, h_part)
-    for side in range(2):
-        @pl.when(sends("gx", side))
-        def _():
-            for i in range(LATE - 1):
-                x_late(side, i).start()
 
     gather(0, c_x, c_out)
 
@@ -406,13 +407,13 @@
         mat[NV - 8 :, :] = pltpu.roll(panel, NV - 8, 1)
         return carry
 
-    lax.fori_loop(0, 9, eliminate, 0)
+    lax.fori_loop(0, 8, eliminate, 0)
     gather(3, h_x, h_out)
     for side in range(2):
         @pl.when(sends("gx", side))
         def _():
             x_late(side, LATE - 1).start()
-    lax.fori_loop(9, 16, eliminate, 0)
+    lax.fori_loop(8, 16, eliminate, 0)
 
     row_of, lane_of = iota((NV, NV), 0), iota((NV, NV), 1)
     one = jnp.where(row_of == lane_of, 1.0, 0.0)
@@ -528,11 +529,15 @@
             dma((6,)),
         ],
         compiler_params=pltpu.CompilerParams(
-            collective_id=0, has_side_effects=True, vmem_limit_bytes=61 * 1024 * 1024
+            collective_id=0, has_side_effects=True, vmem_limit_bytes=55072 * 1024
         ),
     )(subspace, jnp.transpose(potential, (0, 2, 1)))
     density, energy = pl.pallas_call(
-        to_cells, out_shape=(out, out), in_specs=[whole, whole], out_specs=(whole, whole)
+        to_cells,
+        out_shape=(out, out),
+        in_specs=[whole, whole],
+        out_specs=(whole, whole),
+        compiler_params=pltpu.CompilerParams(vmem_limit_bytes=8 * 1024 * 1024),
     )(rows_d, rows_e)
     return jnp.transpose(density, (0, 2, 1)), jnp.transpose(energy, (0, 2, 1))
 

time: 46.2 us -> 44.7 us (0.968)
  Pallas kernels: 45.4 us -> 43.9 us
    pallas_call x1, Pallas kernels: 1.62 us -> 0.8 us  [body(): pl.pallas_call(to_cells, out_shape=(out, out), in_specs=[whole, whole], o...]
    pallas_call x1, Pallas kernels: 43.8 us -> 43.1 us  [body(): pl.pallas_call(functools.partial(kernel, sizes), out_shape=(rows_out, row...]
where the time goes in v5:
time: 44.7 us; the launch traced here: 44.6 us
  Pallas kernels  43.9 us (98%)
  between operations  0.64 us (1%)
    pallas_call x1, Pallas kernels, body(): pl.pallas_call(functools.partial(kernel, sizes), out_shape=(rows_out, row...  43.1 us

profile of v5, /device:TPU:1, one launch (start us, length us, event | category | flops | bytes accessed | tf_op | source)
XLA Modules:
  0.0 44.6 jit_solution(5015499645307037719)
XLA Ops:
  0.6 43.1 %shard_map.41 = (f32[48,256]{1,0:T(8,128)S(1)}, f32[48,256]{1,0:T(8,128)S(1)}) custom-call(bf16[8,48,32,128]{3,2,1,0:T(8,128)(2,1)} %u_hbm.1, f32[8,32,48]{2,1,0:T(8,128)} %bitcast.3), custom_call_target="tpu_custom_call" | custom-call | tf_op jit(solution)/shard_map/pallas_call | solution.py:494
  43.8 0.8 %shard_map.42 = (f32[8,32,48]{2,1,0:T(8,128)}, f32[8,32,48]{2,1,0:T(8,128)}) custom-call(f32[48,256]{1,0:T(8,128)S(1)} %get-tuple-element.6.rows_d, f32[48,256]{1,0:T(8,128)S(1)} %get-tuple-element.7.rows_e), custom_call_target="tpu_custom_call" | custom-call | tf_op jit(solution)/shard_map/pallas_call | solution.py:535

commit v6 on v5

--- a/solution.py
+++ b/solution.py
@@ -18,7 +18,8 @@
 HALF = CY // 2
 LOADS = 2
 PIECES = 4
-LATE = 4
+LATE = 8
+LAST = 2
 ZPIECES = 2
 STACK = 16
 
@@ -185,7 +186,7 @@
     for side in range(2):
         @pl.when(sends("gx", side))
         def _():
-            for n in range(PIECES - 1):
+            for n in range(PIECES):
                 x_early(side, n).start()
 
         @pl.when(sends("gz", side))
@@ -310,19 +311,9 @@
     z_arrived(0)
     apply(0)
     across(0, c_part, c_x)
-    for side in range(2):
-        @pl.when(sends("gx", side))
-        def _():
-            x_early(side, PIECES - 1).start()
     z_arrived(1)
     apply(span)
     product(range(2, span))
-
-    for side in range(2):
-        @pl.when(sends("gx", side))
-        def _():
-            for i in range(LATE - 1):
-                x_late(side, i).start()
 
     for side in range(2):
         @pl.when(receives("gy", side))
@@ -336,6 +327,11 @@
         rounded[far] = appl[far].astype(BF16)
         rounded[near] = appl[near].astype(BF16)
     product([0, 1, *range(span, CY)])
+    for side in range(2):
+        @pl.when(sends("gx", side))
+        def _():
+            for i in range(LATE - LAST):
+                x_late(side, i).start()
 
 
     for i in range(PIECES):
@@ -396,24 +392,24 @@
                 column[t] = column[t] - factor * spread(column[t], s)
         left = jnp.where((lane >= 8) & (lane < NV - 8 * b), panel, 0.0)
         unit = jnp.where(lane < prow, panel, jnp.where(lane == prow, 1.0, 0.0))
-        right = jnp.where(lane < 8, unit, panel) * inverse
+        right = pltpu.roll(jnp.where(lane < 8, unit, panel) * inverse, NV - 8, 1)
         p0, p1, p2 = split(left)
         q0, q1, q2 = split(right)
-        left = jnp.concatenate([p0, p0, p1, p0, p1, p2], axis=0).T.astype(BF16)
+        left = jnp.concatenate([p0, p0, p1, p0, p1, p2], axis=0).astype(BF16).T
         right = jnp.concatenate([q0, q1, q0, q2, q1, q0], axis=0).astype(BF16)
-        rest = jnp.where(outside, mat[...], 0.0) - dot_nn(left, right)
-        rest = pltpu.roll(rest, NV - 8, 1)
+        rest = pltpu.roll(jnp.where(outside, mat[...], 0.0), NV - 8, 1) - dot_nn(left, right)
         mat[0 : NV - 8, :] = rest[8:, :]
         mat[NV - 8 :, :] = pltpu.roll(panel, NV - 8, 1)
         return carry
 
-    lax.fori_loop(0, 8, eliminate, 0)
+    lax.fori_loop(0, 7, eliminate, 0)
     gather(3, h_x, h_out)
     for side in range(2):
         @pl.when(sends("gx", side))
         def _():
-            x_late(side, LATE - 1).start()
-    lax.fori_loop(8, 16, eliminate, 0)
+            for i in range(LATE - LAST, LATE):
+                x_late(side, i).start()
+    lax.fori_loop(7, 16, eliminate, 0)
 
     row_of, lane_of = iota((NV, NV), 0), iota((NV, NV), 1)
     one = jnp.where(row_of == lane_of, 1.0, 0.0)
@@ -432,12 +428,14 @@
 
     lower = linv[...]
     hamil = gathered(3, h_out) * (-1.0 / (24.0 * ncell))
-    reduced = exact_nt(exact(lower, hamil), lower)
-    reduced = 0.5 * (reduced + reduced.T)
-    shifted = reduced - one * (jnp.sum(reduced * one) / NV)
-    sign = shifted * lax.rsqrt(jnp.full((1, 1), jnp.sum(shifted * shifted) + 1e-06, F32))
+    raw = exact_nt(exact(lower, hamil), lower)
+    shifted = 0.5 * (raw + raw.T) - one * (jnp.sum(raw * one) / NV)
+    scale = lax.rsqrt(jnp.full((1, 1), jnp.sum(shifted * shifted) + 1e-06, F32))
+    square = three(shifted, shifted) * (scale * scale)
+    sign = shifted * scale
     for step in range(FILTER_STEPS):
-        square = three(sign, sign)
+        if step > 0:
+            square = three(sign, sign)
         sign = 1.5 * sign - 0.5 * three(square, sign)
     rot = exact(linvt[...], exact(0.5 * (one - sign), lower))
     rot = (0.5 * (rot + rot.T)).astype(BF16)

time: 44.7 us -> 44.3 us (level)
  no operation moved by 1% of the time
where the time goes in v6:
time: 44.3 us; the launch traced here: 44.2 us
  Pallas kernels  43.6 us (98%)
  between operations  0.64 us (1%)
    pallas_call x1, Pallas kernels, body(): pl.pallas_call(functools.partial(kernel, sizes), out_shape=(rows_out, row...  42.8 us

profile of v6, /device:TPU:1, one launch (start us, length us, event | category | flops | bytes accessed | tf_op | source)
XLA Modules:
  0.0 44.2 jit_solution(4239349886626039110)
XLA Ops:
  0.6 42.8 %shard_map.41 = (f32[48,256]{1,0:T(8,128)S(1)}, f32[48,256]{1,0:T(8,128)S(1)}) custom-call(bf16[8,48,32,128]{3,2,1,0:T(8,128)(2,1)} %u_hbm.1, f32[8,32,48]{2,1,0:T(8,128)} %bitcast.3), custom_call_target="tpu_custom_call" | custom-call | tf_op jit(solution)/shard_map/pallas_call | solution.py:492
  43.4 0.8 %shard_map.42 = (f32[8,32,48]{2,1,0:T(8,128)}, f32[8,32,48]{2,1,0:T(8,128)}) custom-call(f32[48,256]{1,0:T(8,128)S(1)} %get-tuple-element.6.rows_d, f32[48,256]{1,0:T(8,128)S(1)} %get-tuple-element.7.rows_e), custom_call_target="tpu_custom_call" | custom-call | tf_op jit(solution)/shard_map/pallas_call | solution.py:533

commit v7 on v6

--- a/solution.py
+++ b/solution.py
@@ -18,8 +18,7 @@
 HALF = CY // 2
 LOADS = 2
 PIECES = 4
-LATE = 8
-LAST = 2
+LATE = (18, 6)
 ZPIECES = 2
 STACK = 16
 
@@ -103,16 +102,16 @@
         peer = lax.rem(gx + 1, nx) if side == 0 else lax.rem(gx + nx - 1, nx)
         return send(
             u_hbm.at[layers, span], hx.at[side, :, span],
-            x_send.at[side, slot], x_recv.at[side, slot], "gx", peer,
+            x_send.at[side], x_recv.at[side, slot], "gx", peer,
         )
 
-    early_n, late_n = HALF // PIECES, HALF // LATE
+    early_n = HALF // PIECES
 
     def x_early(side, i):
         return x_copy(side, (HALF if side == 0 else 0) + i * early_n, early_n, i)
 
     def x_late(side, i):
-        return x_copy(side, (0 if side == 0 else HALF) + i * late_n, late_n, PIECES + i)
+        return x_copy(side, (0 if side == 0 else HALF) + sum(LATE[:i]), LATE[i], PIECES + i)
 
     def y_copy(side):
         layers = pl.ds(CY - 2, 2) if side == 0 else pl.ds(0, 2)
@@ -126,7 +125,7 @@
         peer = lax.rem(gz + 1, nz) if side == 0 else lax.rem(gz + nz - 1, nz)
         return send(
             zs.at[span, side], hz.at[span, side],
-            z_send.at[side, i], z_recv.at[side, i], "gz", peer,
+            z_send.at[side], z_recv.at[side, i], "gz", peer,
         )
 
     def sends(axis, side):
@@ -204,14 +203,14 @@
 
     def post(stage, source, target, peer):
         pltpu.make_async_remote_copy(
-            src_ref=source, dst_ref=target, send_sem=ar_send.at[stage], recv_sem=ar_recv.at[stage],
+            src_ref=source, dst_ref=target, send_sem=ar_send.at[stage // 3], recv_sem=ar_recv.at[stage],
             device_id=peer, device_id_type=MESH,
         ).start()
 
     def finish(stage, like, count):
         whole = like.at[pl.ds(0, count)]
         pltpu.make_async_copy(whole, whole, ar_recv.at[stage]).wait()
-        pltpu.make_async_copy(whole, whole, ar_send.at[stage]).wait()
+        pltpu.make_async_copy(whole, whole, ar_send.at[stage // 3]).wait()
 
     def scatter(base, whole, source, part):
         for i in range(slices):
@@ -330,8 +329,7 @@
     for side in range(2):
         @pl.when(sends("gx", side))
         def _():
-            for i in range(LATE - LAST):
-                x_late(side, i).start()
+            x_late(side, 0).start()
 
 
     for i in range(PIECES):
@@ -407,8 +405,7 @@
     for side in range(2):
         @pl.when(sends("gx", side))
         def _():
-            for i in range(LATE - LAST, LATE):
-                x_late(side, i).start()
+            x_late(side, 1).start()
     lax.fori_loop(7, 16, eliminate, 0)
 
     row_of, lane_of = iota((NV, NV), 0), iota((NV, NV), 1)
@@ -419,7 +416,7 @@
     linv[...] = lower
     linvt[...] = lower.T
 
-    for i in range(LATE):
+    for i in range(len(LATE)):
         for side in range(2):
             @pl.when(receives("gx", side))
             def _():
@@ -454,10 +451,7 @@
     for side in range(2):
         @pl.when(sends("gx", side))
         def _():
-            for i in range(PIECES):
-                x_early(side, i).wait_send()
-            for i in range(LATE):
-                x_late(side, i).wait_send()
+            x_copy(side, 0, CY, 0).wait_send()
 
         @pl.when(sends("gy", side))
         def _():
@@ -465,8 +459,8 @@
 
         @pl.when(sends("gz", side))
         def _():
-            for i in range(ZPIECES):
-                z_copy(side, i).wait_send()
+            whole = zs.at[:, side]
+            pltpu.make_async_copy(whole, whole, z_send.at[side]).wait()
 
 
 def to_cells(rows_d, rows_e, density, energy):
@@ -517,13 +511,13 @@
             vm((NV, NV), F32),
             vm((NV, NV), F32),
             dma((LOADS + 1,)),
-            dma((2, PIECES + LATE)),
-            dma((2, PIECES + LATE)),
+            dma((2,)),
+            dma((2, PIECES + len(LATE))),
+            dma((2,)),
             dma((2,)),
             dma((2,)),
             dma((2, ZPIECES)),
-            dma((2, ZPIECES)),
-            dma((6,)),
+            dma((2,)),
             dma((6,)),
         ],
         compiler_params=pltpu.CompilerParams(

time: 44.3 us -> 43.9 us (level)
  no operation moved by 1% of the time
where the time goes in v7:
time: 43.9 us; the launch traced here: 43.8 us
  Pallas kernels  43.2 us (98%)
  between operations  0.64 us (1%)
    pallas_call x1, Pallas kernels, body(): pl.pallas_call(functools.partial(kernel, sizes), out_shape=(rows_out, row...  42.4 us

profile of v7, /device:TPU:1, one launch (start us, length us, event | category | flops | bytes accessed | tf_op | source)
XLA Modules:
  0.0 43.8 jit_solution(16034599925832904588)
XLA Ops:
  0.6 42.4 %shard_map.41 = (f32[48,256]{1,0:T(8,128)S(1)}, f32[48,256]{1,0:T(8,128)S(1)}) custom-call(bf16[8,48,32,128]{3,2,1,0:T(8,128)(2,1)} %u_hbm.1, f32[8,32,48]{2,1,0:T(8,128)} %bitcast.3), custom_call_target="tpu_custom_call" | custom-call | tf_op jit(solution)/shard_map/pallas_call | solution.py:486
  43.0 0.8 %shard_map.42 = (f32[8,32,48]{2,1,0:T(8,128)}, f32[8,32,48]{2,1,0:T(8,128)}) custom-call(f32[48,256]{1,0:T(8,128)S(1)} %get-tuple-element.6.rows_d, f32[48,256]{1,0:T(8,128)S(1)} %get-tuple-element.7.rows_e), custom_call_target="tpu_custom_call" | custom-call | tf_op jit(solution)/shard_map/pallas_call | solution.py:527

commit v8 on v7

--- a/solution.py
+++ b/solution.py
@@ -18,7 +18,7 @@
 HALF = CY // 2
 LOADS = 2
 PIECES = 4
-LATE = (18, 6)
+LATE = (20, 4)
 ZPIECES = 2
 STACK = 16
 

time: 43.9 us -> 43.9 us (level)
  no operation moved by 1% of the time
where the time goes in v8:
time: 43.9 us; the launch traced here: 43.8 us
  Pallas kernels  43.2 us (98%)
  between operations  0.64 us (1%)
    pallas_call x1, Pallas kernels, body(): pl.pallas_call(functools.partial(kernel, sizes), out_shape=(rows_out, row...  42.4 us

profile of v8, /device:TPU:1, one launch (start us, length us, event | category | flops | bytes accessed | tf_op | source)
XLA Modules:
  0.0 43.8 jit_solution(15573930832957561204)
XLA Ops:
  0.6 42.4 %shard_map.41 = (f32[48,256]{1,0:T(8,128)S(1)}, f32[48,256]{1,0:T(8,128)S(1)}) custom-call(bf16[8,48,32,128]{3,2,1,0:T(8,128)(2,1)} %u_hbm.1, f32[8,32,48]{2,1,0:T(8,128)} %bitcast.3), custom_call_target="tpu_custom_call" | custom-call | tf_op jit(solution)/shard_map/pallas_call | solution.py:486
  43.0 0.8 %shard_map.42 = (f32[8,32,48]{2,1,0:T(8,128)}, f32[8,32,48]{2,1,0:T(8,128)}) custom-call(f32[48,256]{1,0:T(8,128)S(1)} %get-tuple-element.6.rows_d, f32[48,256]{1,0:T(8,128)S(1)} %get-tuple-element.7.rows_e), custom_call_target="tpu_custom_call" | custom-call | tf_op jit(solution)/shard_map/pallas_call | solution.py:527
